TPU v7x, 256 devices: a whole 4x4x8 slice. The times are simulated.
256 devices in a mesh: seq: 128 (over y, z, x_hi, core), head: 2 (over x_lo).
Axes of the slice: x: 4 (x_hi: 2, x_lo: 2; x = x_hi * 2 + x_lo), y: 4, z: 8, core: 2. Of those that a mesh axis runs over, the one named last changes fastest.
Arguments:
- queries: bfloat16 [32768, 2048], P(('seq', 'head')), may hold values from -28 to 28
- key_states: bfloat16 [32768, 512], P(('seq', 'head')), may hold values from -20 to 20
- value_vector_rows: bfloat16 [32768, 512], P(('seq', 'head')), may hold values from -6 to 6
- grad_output: bfloat16 [32768, 2048], P(('seq', 'head')), may hold values from -6 to 6
- doc_ids: int32 [256], replicated, may hold values from 0 to 31, never falling along the last dimension, each value on 1 to 64 neighbouring positions
- block_home: int32 [256], replicated, may hold values from 0 to 255, as said below
Outputs:
- attended: bfloat16 [32768, 2048], P('seq', 'head')
- grad_query: bfloat16 [32768, 2048], P('seq', 'head')
- key_gradient: bfloat16 [32768, 512], P('seq', 'head')
- value_gradient: bfloat16 [32768, 512], P('seq', 'head')
Inputs may be any that keep to these rules, and one draw needn't show every extreme that they name: `block_home`: a permutation of the natural blocks; slots are numbered shard by shard, 2 slots to a seq shard; every block sits in its natural shard (block // 2) or one beside it, and across each boundary between neighbouring shards exactly one block moves each way.
All inputs are finite; a program needn't handle non-finite values.
Results may differ from a plain program's by a relative error of at most 0.025.
Values may be sent and summed in bfloat16 or wider, within the bound.
A program may use at most 192 MiB of HBM per device.

v0:
```python
import math

import jax
import jax.numpy as jnp
from jax import lax
from jax.sharding import PartitionSpec as P

BLK = 128
WINDOW = 2048
HEAD_SIZE = 128


def with_halo(cells, sides, width):
    for axis, dim in sides:
        count = lax.axis_size(axis)
        ends = count - 1
        head = lax.slice_in_dim(cells, 0, width, axis=dim)
        tail = lax.slice_in_dim(cells, cells.shape[dim] - width, cells.shape[dim], axis=dim)
        cells = jnp.concatenate(
            [
                lax.ppermute(tail, axis, [(i, (i + 1) % count) for i in range(ends)]),
                cells,
                lax.ppermute(head, axis, [((i + 1) % count, i) for i in range(ends)]),
            ],
            axis=dim,
        )
    return cells


def passed_along(block, axis, distance):
    devices = range(lax.axis_size(axis))
    route = [(i - distance, i) for i in devices if i - distance in devices]
    return lax.ppermute(block, axis, route)


def per_device(queries, key_states, value_vector_rows, grad_output, doc_ids, block_home):
    seq_at = lax.axis_index("seq")
    arrived = (
        lax.all_to_all(queries, "head", split_axis=1, concat_axis=0, tiled=True),
        lax.all_to_all(key_states, "head", split_axis=1, concat_axis=0, tiled=True),
        lax.all_to_all(value_vector_rows, "head", split_axis=1, concat_axis=0, tiled=True),
        lax.all_to_all(grad_output, "head", split_axis=1, concat_axis=0, tiled=True),
    )
    tokens_dev = arrived[0].shape[0]
    block_count = tokens_dev // BLK
    widths_list = [member.shape[1] for member in arrived]
    packed = jnp.concatenate(list(arrived), axis=1)
    width_all = packed.shape[1]
    block_total = doc_ids.shape[0]
    listing = jnp.arange(block_total, dtype=jnp.int32)
    wanted = seq_at * block_count + jnp.arange(block_count, dtype=jnp.int32)
    owners = jnp.sum(jnp.where(block_home[None, :] == wanted[:, None], listing[None, :], 0), axis=1)
    beside_all = with_halo(packed, (("seq", 0),), tokens_dev)
    offsets = (owners - (seq_at - 1) * block_count) * BLK
    natural = jax.vmap(lambda first_row: lax.dynamic_slice_in_dim(beside_all, first_row, BLK, 0))(
        offsets
    ).reshape(tokens_dev, width_all)
    edge_one = widths_list[0]
    edge_two = edge_one + widths_list[1]
    edge_three = edge_two + widths_list[2]
    query_natural_order = natural[:, :edge_one]
    key_natural_order = natural[:, edge_one:edge_two]
    value_natural_order = natural[:, edge_two:edge_three]
    gradient_natural_order = natural[:, edge_three:]
    kv_heads = key_natural_order.shape[1] // HEAD_SIZE
    queries_per_group = query_natural_order.shape[1] // key_natural_order.shape[1]
    key_width = kv_heads * HEAD_SIZE
    reciprocal_root = 1.0 / math.sqrt(HEAD_SIZE)
    query_four = query_natural_order.reshape(tokens_dev, kv_heads, queries_per_group, HEAD_SIZE)
    grad_four = gradient_natural_order.reshape(tokens_dev, kv_heads, queries_per_group, HEAD_SIZE)
    key_value = jnp.concatenate([key_natural_order, value_natural_order], axis=1)
    reach = WINDOW // tokens_dev
    tails = [passed_along(key_value, "seq", back) for back in range(1, reach + 1)]
    stacked = jnp.stack([key_value] + tails)
    padded_doc = jnp.concatenate([jnp.full((reach * block_count,), -1, jnp.int32), doc_ids])
    distances = jnp.arange(reach + 1, dtype=jnp.int32)
    key_docs = jax.vmap(
        lambda back: jnp.repeat(
            lax.dynamic_slice_in_dim(
                padded_doc, (seq_at - back + reach) * block_count, block_count, 0
            ),
            BLK,
        )
    )(distances)
    query_doc = jnp.repeat(
        lax.dynamic_slice_in_dim(doc_ids, seq_at * block_count, block_count, 0), BLK
    )
    positions = jnp.arange(tokens_dev, dtype=jnp.int32)

    def visible_of(back, key_doc):
        distance = back * tokens_dev + positions[:, None] - positions[None, :]
        return (query_doc[:, None] == key_doc[None, :]) & (distance >= 0) & (distance < WINDOW)

    def split_block(block):
        local_keys = block[:, :key_width].reshape(tokens_dev, kv_heads, HEAD_SIZE)
        local_values = block[:, key_width:].reshape(tokens_dev, kv_heads, HEAD_SIZE)
        return (local_keys, local_values)

    visible_all = jax.vmap(visible_of)(distances, key_docs)

    def score_pass(carried, entry):
        block, visible = entry
        local_keys, local_values = split_block(block)
        kept = (
            jnp.einsum("tgqd,ugd->gqtu", query_four, local_keys, preferred_element_type=jnp.float32)
            * reciprocal_root
        )
        return (carried, kept)

    unused_one, scores_all = lax.scan(score_pass, 0, (stacked, visible_all))
    seen = visible_all[:, None, None, :, :]
    final_max = jnp.max(jnp.where(seen, scores_all, -1e30), axis=(0, 4))
    final_sum = jnp.sum(
        jnp.where(seen, jnp.exp(scores_all - final_max[None, ..., None]), 0.0), axis=(0, 4)
    )
    log_total = final_max + jnp.log(final_sum)

    def second_pass(carried, entry):
        block, visible, scores = entry
        local_keys, local_values = split_block(block)
        probability_lowered = jnp.where(
            visible, jnp.exp(scores - log_total[..., None]), 0.0
        ).astype(jnp.bfloat16)
        return (
            carried
            + jnp.einsum(
                "gqtu,ugd->tgqd",
                probability_lowered,
                local_values,
                preferred_element_type=jnp.float32,
            ),
            None,
        )

    out_start = jnp.zeros((tokens_dev, kv_heads, queries_per_group, HEAD_SIZE), jnp.float32)
    out_accum, unused_two = lax.scan(second_pass, out_start, (stacked, visible_all, scores_all))
    attended = out_accum.astype(jnp.bfloat16)
    delta = jnp.einsum("tgqd,tgqd->gqt", grad_four, attended, preferred_element_type=jnp.float32)

    def gradients(block, visible, scores):
        local_keys, local_values = split_block(block)
        prob = jnp.where(visible, jnp.exp(scores - log_total[..., None]), 0.0)
        probability_lowered = prob.astype(jnp.bfloat16)
        grad_prob = jnp.einsum(
            "tgqd,ugd->gqtu", grad_four, local_values, preferred_element_type=jnp.float32
        )
        score_gradient = (prob * (grad_prob - delta[..., None])).astype(jnp.bfloat16)
        query_term = jnp.einsum(
            "gqtu,ugd->tgqd", score_gradient, local_keys, preferred_element_type=jnp.float32
        )
        key_contribution = jnp.einsum(
            "nzev,enzx->vnx", score_gradient, query_four, preferred_element_type=jnp.float32
        ).reshape(tokens_dev, key_width)
        value_contribution = jnp.einsum(
            "nzev,enzx->vnx", probability_lowered, grad_four, preferred_element_type=jnp.float32
        ).reshape(tokens_dev, key_width)
        return (query_term, jnp.concatenate([key_contribution, value_contribution], axis=1))

    query_accum, dkv_total = gradients(stacked[0], visible_all[0], scores_all[0])
    for back in range(1, reach + 1):
        query_term, shard_term = gradients(stacked[back], visible_all[back], scores_all[back])
        query_accum = query_accum + query_term
        dkv_total = dkv_total + passed_along(shard_term.astype(jnp.bfloat16), "seq", -back).astype(
            shard_term.dtype
        )
    attended_out = attended.reshape(tokens_dev, kv_heads * queries_per_group * HEAD_SIZE)
    grad_query = (
        (query_accum * reciprocal_root)
        .astype(jnp.bfloat16)
        .reshape(tokens_dev, kv_heads * queries_per_group * HEAD_SIZE)
    )
    key_gradient = (dkv_total[:, :key_width] * reciprocal_root).astype(jnp.bfloat16)
    value_gradient = dkv_total[:, key_width:].astype(jnp.bfloat16)
    return (attended_out, grad_query, key_gradient, value_gradient)


def solution(mesh):
    return jax.shard_map(
        per_device,
        mesh=mesh,
        in_specs=(
            P(("seq", "head"), None),
            P(("seq", "head"), None),
            P(("seq", "head"), None),
            P(("seq", "head"), None),
            P(),
            P(),
        ),
        out_specs=(P("seq", "head"), P("seq", "head"), P("seq", "head"), P("seq", "head")),
        check_vma=False,
    )
```

profile of v0, /device:TPU:40, one launch (start us, length us, event | category | flops | bytes accessed | tf_op | source)
XLA Modules:
  0.0 436.9 jit_solution(14518422073520038242)
XLA Ops:
  2.3 3.4 all-to-all-start.1
  7.2 2.9 all-to-all-done.1
  10.1 3.4 all-to-all-start.2
  15.4 2.6 all-to-all-done.2
  18.0 3.5 all-to-all-start.3
  22.5 5.5 %all-to-all-done.3 = bf16[128,2,1024]{2,0,1:T(8,128)(2,1)S(1)} async-done(((bf16[128,2,1024]{2,0,1:T(8,128)(2,1)}), bf16[128,2,1024]{2,0,1:T(8,128)(2,1)S(1)}, u32[]{:S(2)}, u32[]{:S(2)}) %all-to-all-start.3) | async-done | bytes 524320 | tf_op jit(solution)/shard_map/all_to_all | solution.py:42
  28.0 3.5 all-to-all-start
  32.5 5.6 %all-to-all-done = bf16[128,2,1024]{2,0,1:T(8,128)(2,1)S(1)} async-done(((bf16[128,2,1024]{2,0,1:T(8,128)(2,1)}), bf16[128,2,1024]{2,0,1:T(8,128)(2,1)S(1)}, u32[]{:S(2)}, u32[]{:S(2)}) %all-to-all-start) | async-done | bytes 524320 | tf_op jit(solution)/shard_map/all_to_all | solution.py:39
  41.2 6.0 %collective-permute-start.1 = (bf16[256,2560]{1,0:T(8,128)(2,1)}, bf16[256,2560]{1,0:T(8,128)(2,1)}, u32[]{:S(2)}, u32[]{:S(2)}) collective-permute-start(bf16[256,2560]{1,0:T(8,128)(2,1)} %pad_maximum_fusion.1), channel_id=1, source_target_pairs={{2,0},{4,2},{6,4},{8,6},{10,8},{12,10},{14,12},{16,14},{18,16},{20... | collective-permute-start | bytes 3932168 | tf_op jit(solution)/shard_map/ppermute | solution.py:23
  56.3 4.7 %collective-permute-done = bf16[256,2560]{1,0:T(8,128)(2,1)} collective-permute-done((bf16[256,2560]{1,0:T(8,128)(2,1)}, bf16[256,2560]{1,0:T(8,128)(2,1)}, u32[]{:S(2)}, u32[]{:S(2)}) %collective-permute-start) | collective-permute-done | bytes 1310752 | tf_op jit(solution)/shard_map/ppermute | solution.py:21
  62.7 3.7 pad_maximum_fusion
  66.3 4.3 while.26
  68.5 2.2 bitcast_dynamic-update-slice_fusion.16
  72.5 14.0 %collective-permute-start.2 = (bf16[256,512]{0,1:T(8,128)(2,1)}, bf16[256,512]{0,1:T(8,128)(2,1)}, u32[]{:S(2)}, u32[]{:S(2)}) collective-permute-start(bf16[256,512]{0,1:T(8,128)(2,1)} %copy.360), channel_id=1, source_target_pairs={{0,2},{2,4},{4,6},{6,8},{8,10},{10,12},{12,14},{14,16},{16,18},{18... | collective-permute-start | bytes 786440 | tf_op jit(solution)/shard_map/ppermute | solution.py:33
  86.5 4.2 collective-permute-start.3
  90.7 6.2 %collective-permute-start.4 = (bf16[256,512]{0,1:T(8,128)(2,1)}, bf16[256,512]{0,1:T(8,128)(2,1)}, u32[]{:S(2)}, u32[]{:S(2)}) collective-permute-start(bf16[256,512]{0,1:T(8,128)(2,1)} %copy.360), channel_id=1, source_target_pairs={{0,6},{2,8},{4,10},{6,12},{8,14},{10,16},{12,18},{14,20},{16,22},{... | collective-permute-start | bytes 786440 | tf_op jit(solution)/shard_map/ppermute | solution.py:33
  96.9 3.8 collective-permute-start.5
  109.8 5.0 %collective-permute-start.7 = (bf16[256,512]{0,1:T(8,128)(2,1)}, bf16[256,512]{0,1:T(8,128)(2,1)S(1)}, u32[]{:S(2)}, u32[]{:S(2)}) collective-permute-start(bf16[256,512]{0,1:T(8,128)(2,1)} %copy.360), channel_id=1, source_target_pairs={{0,12},{2,14},{4,16},{6,18},{8,20},{10,22},{12,24},{14,26},{16,28}... | collective-permute-start | bytes 786440 | tf_op jit(solution)/shard_map/ppermute | solution.py:33
  116.5 5.8 %collective-permute-start.8 = (bf16[256,512]{0,1:T(8,128)(2,1)}, bf16[256,512]{0,1:T(8,128)(2,1)S(1)}, u32[]{:S(2)}, u32[]{:S(2)}) collective-permute-start(bf16[256,512]{0,1:T(8,128)(2,1)} %copy.360), channel_id=1, source_target_pairs={{0,14},{2,16},{4,18},{6,20},{8,22},{10,24},{12,26},{14,28},{16,30}... | collective-permute-start | bytes 786440 | tf_op jit(solution)/shard_map/ppermute | solution.py:33
  130.2 19.6 %collective-permute-done.7 = bf16[256,512]{0,1:T(8,128)(2,1)S(1)} collective-permute-done((bf16[256,512]{0,1:T(8,128)(2,1)}, bf16[256,512]{0,1:T(8,128)(2,1)S(1)}, u32[]{:S(2)}, u32[]{:S(2)}) %collective-permute-start.7) | collective-permute-done | bytes 262176 | tf_op jit(solution)/shard_map/ppermute | solution.py:33
  152.1 25.4 %while.25 = (s32[]{:T(128)}, f32[9,2,4,256,256]{3,4,2,1,0:T(8,128)}, bf16[9,256,512]{1,2,0:T(8,128)(2,1)}, bf16[256,2,4,128]{3,0,2,1:T(8,128)(2,1)S(1)}) while((s32[]{:T(128)}, f32[9,2,4,256,256]{3,4,2,1,0:T(8,128)}, bf16[9,256,512]{1,2,0:T(8,128)(2,1)}, bf16[256,2,4,128]{3,0,2,1:T(8,128)(2,1)S(1)}) %tuple.94), condition=%wide.region_2.3_spmd.clone, body=%wide.region_1.2_spmd.sunk.clone | while | flops 134742016 | bytes 3539513 | solution.py:110
  177.5 8.7 %select_reduce_fusion.1 = f32[2,4,256]{2,1,0:T(4,128)S(1)} fusion(f32[9,2,4,256,256]{3,4,2,1,0:T(8,128)} %get-tuple-element.354, pred[9,256,256]{1,2,0:T(8,128)(4,1)S(1)} %copy.180), kind=kLoop, calls=%fused_computation.20 | loop fusion | flops 9435136 | bytes 19472384 | tf_op jit(solution)/shard_map/reduce_max | solution.py:112
  186.1 9.6 %select_reduce_fusion = f32[2,4,256]{2,1,0:T(4,128)S(1)} fusion(f32[9,2,4,256,256]{3,4,2,1,0:T(8,128)} %get-tuple-element.354, f32[2,4,256]{2,1,0:T(4,128)S(1)} %select_reduce_fusion.1, pred[9,256,256]{1,2,0:T(8,128)(4,1)S(1)} %copy.180), kind=kLoop, calls=%fused_computation.19 | loop fusion | flops 14153728 | bytes 19480576 | tf_op jit(solution)/shard_map/reduce_sum | solution.py:113
  195.7 77.9 %while.27 = (s32[]{:T(128)}, f32[256,2,4,128]{0,3,2,1:T(8,128)}, bf16[9,256,512]{1,2,0:T(8,128)(2,1)}, pred[9,256,256]{2,1,0:T(8,128)(4,1)S(1)}, f32[9,2,4,256,256]{3,4,2,1,0:T(8,128)}, /*index=5*/f32[2,4,256]{2,1,0:T(4,128)S(1)}) while((s32[]{:T(128)}, f32[256,2,4,128]{0,3,2,1:T(8,128)}, ...), condition=%wide.region_6.7_spmd.clone.clone, body=%wide.region_5.6_spmd.clone.sunk.clone | while | flops 136314880 | bytes 13705307 | solution.py:136
  195.7 3.1 constant_dynamic-slice_fusion.7
  203.3 3.1 constant_dynamic-slice_fusion.7
  209.3 2.8 fusion.238
  212.1 3.1 constant_dynamic-slice_fusion.7
  218.1 2.8 fusion.238
  220.9 3.1 constant_dynamic-slice_fusion.7
  226.9 2.8 fusion.238
  229.7 3.1 constant_dynamic-slice_fusion.7
  235.7 2.8 fusion.238
  238.5 3.1 constant_dynamic-slice_fusion.7
  244.5 2.8 fusion.238
  247.3 3.1 constant_dynamic-slice_fusion.7
  253.3 2.8 fusion.238
  256.1 3.1 constant_dynamic-slice_fusion.7
  262.1 2.8 fusion.238
  264.9 3.1 constant_dynamic-slice_fusion.7
  270.9 2.8 fusion.238
  273.7 2.4 fusion.92
  279.7 2.2 fusion.42
  285.3 2.8 fusion.69
  289.1 2.3 fusion.38
  299.4 2.3 fusion.34
  305.6 9.7 %collective-permute-start.12 = (bf16[256,512]{1,0:T(8,128)(2,1)}, bf16[256,512]{1,0:T(8,128)(2,1)}, u32[]{:S(2)}, u32[]{:S(2)}) collective-permute-start(bf16[256,512]{1,0:T(8,128)(2,1)} %pad_maximum_fusion.4), channel_id=1, source_target_pairs={{6,0},{8,2},{10,4},{12,6},{14,8},{16,10},{18,12},{20,14},{22,16},{... | collective-permute-start | bytes 786440 | tf_op jit(solution)/shard_map/ppermute | solution.py:33
  319.8 2.2 fusion.30
  326.0 2.4 collective-permute-start.13
  328.4 2.8 fusion.75
  333.5 2.3 fusion.26
  339.7 8.2 %collective-permute-start.14 = (bf16[256,512]{1,0:T(8,128)(2,1)}, bf16[256,512]{1,0:T(8,128)(2,1)}, u32[]{:S(2)}, u32[]{:S(2)}) collective-permute-start(bf16[256,512]{1,0:T(8,128)(2,1)} %pad_maximum_fusion.6), channel_id=1, source_target_pairs={{10,0},{12,2},{14,4},{16,6},{18,8},{20,10},{22,12},{24,14},{26,16}... | collective-permute-start | bytes 786440 | tf_op jit(solution)/shard_map/ppermute | solution.py:33
  347.9 2.8 fusion.77
  353.0 2.3 fusion.22
  359.1 2.8 fusion.79
  364.2 2.2 fusion.18
  370.4 2.8 fusion.81
  375.5 2.2 fusion.14
  380.0 2.8 fusion.90
  382.8 2.2 fusion.46
  395.8 4.5 %collective-permute-start.15 = (bf16[256,512]{1,0:T(8,128)(2,1)}, bf16[256,512]{1,0:T(8,128)(2,1)S(1)}, u32[]{:S(2)}, u32[]{:S(2)}) collective-permute-start(bf16[256,512]{1,0:T(8,128)(2,1)} %pad_maximum_fusion.7), channel_id=1, source_target_pairs={{12,0},{14,2},{16,4},{18,6},{20,8},{22,10},{24,12},{26,14},{28,16}... | collective-permute-start | bytes 786440 | tf_op jit(solution)/shard_map/ppermute | solution.py:33
  406.7 15.4 %collective-permute-done.15 = bf16[256,512]{1,0:T(8,128)(2,1)S(1)} collective-permute-done((bf16[256,512]{1,0:T(8,128)(2,1)}, bf16[256,512]{1,0:T(8,128)(2,1)S(1)}, u32[]{:S(2)}, u32[]{:S(2)}) %collective-permute-start.15) | collective-permute-done | bytes 262176 | tf_op jit(solution)/shard_map/ppermute | solution.py:33
  422.1 6.4 %collective-permute-done.16 = bf16[256,512]{1,0:T(8,128)(2,1)S(1)} collective-permute-done((bf16[256,512]{1,0:T(8,128)(2,1)}, bf16[256,512]{1,0:T(8,128)(2,1)S(1)}, u32[]{:S(2)}, u32[]{:S(2)}) %collective-permute-start.16) | collective-permute-done | bytes 262176 | tf_op jit(solution)/shard_map/ppermute | solution.py:33
  428.6 5.4 %collective-permute-done.17 = bf16[256,512]{1,0:T(8,128)(2,1)S(1)} collective-permute-done((bf16[256,512]{1,0:T(8,128)(2,1)}, bf16[256,512]{1,0:T(8,128)(2,1)S(1)}, u32[]{:S(2)}, u32[]{:S(2)}) %collective-permute-start.17) | collective-permute-done | bytes 262176 | tf_op jit(solution)/shard_map/ppermute | solution.py:33
  (292 shorter events, 170.0 us)
Async XLA Ops:
  0.6 20.8 %copy-start.23 = (bf16[128,2048]{1,0:T(8,128)(2,1)S(1)}, bf16[128,2048]{1,0:T(8,128)(2,1)}, u32[]{:S(2)}) copy-start(bf16[128,2048]{1,0:T(8,128)(2,1)} %param.10) | copy-start | bytes 1572868
  0.6 21.7 %copy-start.42 = (s32[256]{0:T(256)S(1)}, s32[256]{0:T(256)}, u32[]{:S(2)}) copy-start(s32[256]{0:T(256)} %param.15) | copy-start | bytes 3076
  2.3 7.8 %all-to-all-start.1 = ((bf16[128,2,256]{2,0,1:T(8,128)(2,1)}), bf16[128,2,256]{2,0,1:T(8,128)(2,1)S(1)}, u32[]{:S(2)}, u32[]{:S(2)}) async-start(bf16[128,2,256]{2,0,1:T(8,128)(2,1)} %bitcast.573), calls=%async_computation.1 | async-start | bytes 262144 | tf_op jit(solution)/shard_map/all_to_all | solution.py:40
  10.1 7.8 %all-to-all-start.2 = ((bf16[128,2,256]{2,0,1:T(8,128)(2,1)}), bf16[128,2,256]{2,0,1:T(8,128)(2,1)S(1)}, u32[]{:S(2)}, u32[]{:S(2)}) async-start(bf16[128,2,256]{2,0,1:T(8,128)(2,1)} %bitcast.572), calls=%async_computation.2 | async-start | bytes 262144 | tf_op jit(solution)/shard_map/all_to_all | solution.py:41
  13.5 18.2 %copy-start.41 = (s32[256]{0:T(256)S(1)}, s32[256]{0:T(256)}, u32[]{:S(2)}) copy-start(s32[256]{0:T(256)} %param.14) | copy-start | bytes 3076
  18.0 10.1 %all-to-all-start.3 = ((bf16[128,2,1024]{2,0,1:T(8,128)(2,1)}), bf16[128,2,1024]{2,0,1:T(8,128)(2,1)S(1)}, u32[]{:S(2)}, u32[]{:S(2)}) async-start(bf16[128,2,1024]{2,0,1:T(8,128)(2,1)} %bitcast.570), calls=%async_computation.3 | async-start | bytes 1048576 | tf_op jit(solution)/shard_map/all_to_all | solution.py:42
  28.0 10.1 %all-to-all-start = ((bf16[128,2,1024]{2,0,1:T(8,128)(2,1)}), bf16[128,2,1024]{2,0,1:T(8,128)(2,1)S(1)}, u32[]{:S(2)}, u32[]{:S(2)}) async-start(bf16[128,2,1024]{2,0,1:T(8,128)(2,1)} %bitcast.571), calls=%async_computation | async-start | bytes 1048576 | tf_op jit(solution)/shard_map/all_to_all | solution.py:39
  39.2 21.7 %collective-permute-start = (bf16[256,2560]{1,0:T(8,128)(2,1)}, bf16[256,2560]{1,0:T(8,128)(2,1)}, u32[]{:S(2)}, u32[]{:S(2)}) collective-permute-start(bf16[256,2560]{1,0:T(8,128)(2,1)} %pad_maximum_fusion.1), channel_id=1, source_target_pairs={{0,2},{2,4},{4,6},{6,8},{8,10},{10,12},{12,14},{14,16},{16,18},{18... | collective-permute-start | bytes 3932168 | tf_op jit(solution)/shard_map/ppermute | solution.py:21
  41.2 21.5 %collective-permute-start.1 = (bf16[256,2560]{1,0:T(8,128)(2,1)}, bf16[256,2560]{1,0:T(8,128)(2,1)}, u32[]{:S(2)}, u32[]{:S(2)}) collective-permute-start(bf16[256,2560]{1,0:T(8,128)(2,1)} %pad_maximum_fusion.1), channel_id=1, source_target_pairs={{2,0},{4,2},{6,4},{8,6},{10,8},{12,10},{14,12},{16,14},{18,16},{20... | collective-permute-start | bytes 3932168 | tf_op jit(solution)/shard_map/ppermute | solution.py:23
  51.0 234.4 %copy-start.40 = (pred[256,256]{0,1:T(8,128)(4,1)}, pred[256,256]{0,1:T(8,128)(4,1)S(1)}, u32[]{:S(2)}) copy-start(pred[256,256]{0,1:T(8,128)(4,1)S(1)} %copy.191) | copy-start | bytes 196612
  72.5 37.3 %collective-permute-start.2 = (bf16[256,512]{0,1:T(8,128)(2,1)}, bf16[256,512]{0,1:T(8,128)(2,1)}, u32[]{:S(2)}, u32[]{:S(2)}) collective-permute-start(bf16[256,512]{0,1:T(8,128)(2,1)} %copy.360), channel_id=1, source_target_pairs={{0,2},{2,4},{4,6},{6,8},{8,10},{10,12},{12,14},{14,16},{16,18},{18... | collective-permute-start | bytes 786440 | tf_op jit(solution)/shard_map/ppermute | solution.py:33
  86.5 30.0 %collective-permute-start.3 = (bf16[256,512]{0,1:T(8,128)(2,1)}, bf16[256,512]{0,1:T(8,128)(2,1)}, u32[]{:S(2)}, u32[]{:S(2)}) collective-permute-start(bf16[256,512]{0,1:T(8,128)(2,1)} %copy.360), channel_id=1, source_target_pairs={{0,4},{2,6},{4,8},{6,10},{8,12},{10,14},{12,16},{14,18},{16,20},{1... | collective-permute-start | bytes 786440 | tf_op jit(solution)/shard_map/ppermute | solution.py:33
  90.7 33.3 %collective-permute-start.4 = (bf16[256,512]{0,1:T(8,128)(2,1)}, bf16[256,512]{0,1:T(8,128)(2,1)}, u32[]{:S(2)}, u32[]{:S(2)}) collective-permute-start(bf16[256,512]{0,1:T(8,128)(2,1)} %copy.360), channel_id=1, source_target_pairs={{0,6},{2,8},{4,10},{6,12},{8,14},{10,16},{12,18},{14,20},{16,22},{... | collective-permute-start | bytes 786440 | tf_op jit(solution)/shard_map/ppermute | solution.py:33
  96.9 30.8 %collective-permute-start.5 = (bf16[256,512]{0,1:T(8,128)(2,1)}, bf16[256,512]{0,1:T(8,128)(2,1)}, u32[]{:S(2)}, u32[]{:S(2)}) collective-permute-start(bf16[256,512]{0,1:T(8,128)(2,1)} %copy.360), channel_id=1, source_target_pairs={{0,8},{2,10},{4,12},{6,14},{8,16},{10,18},{12,20},{14,22},{16,24},... | collective-permute-start | bytes 786440 | tf_op jit(solution)/shard_map/ppermute | solution.py:33
  100.8 28.6 %collective-permute-start.6 = (bf16[256,512]{0,1:T(8,128)(2,1)}, bf16[256,512]{0,1:T(8,128)(2,1)S(1)}, u32[]{:S(2)}, u32[]{:S(2)}) collective-permute-start(bf16[256,512]{0,1:T(8,128)(2,1)} %copy.360), channel_id=1, source_target_pairs={{0,10},{2,12},{4,14},{6,16},{8,18},{10,20},{12,22},{14,24},{16,26}... | collective-permute-start | bytes 786440 | tf_op jit(solution)/shard_map/ppermute | solution.py:33
  109.8 39.9 %collective-permute-start.7 = (bf16[256,512]{0,1:T(8,128)(2,1)}, bf16[256,512]{0,1:T(8,128)(2,1)S(1)}, u32[]{:S(2)}, u32[]{:S(2)}) collective-permute-start(bf16[256,512]{0,1:T(8,128)(2,1)} %copy.360), channel_id=1, source_target_pairs={{0,12},{2,14},{4,16},{6,18},{8,20},{10,22},{12,24},{14,26},{16,28}... | collective-permute-start | bytes 786440 | tf_op jit(solution)/shard_map/ppermute | solution.py:33
  116.5 34.0 %collective-permute-start.8 = (bf16[256,512]{0,1:T(8,128)(2,1)}, bf16[256,512]{0,1:T(8,128)(2,1)S(1)}, u32[]{:S(2)}, u32[]{:S(2)}) collective-permute-start(bf16[256,512]{0,1:T(8,128)(2,1)} %copy.360), channel_id=1, source_target_pairs={{0,14},{2,16},{4,18},{6,20},{8,22},{10,24},{12,26},{14,28},{16,30}... | collective-permute-start | bytes 786440 | tf_op jit(solution)/shard_map/ppermute | solution.py:33
  124.0 27.3 %collective-permute-start.9 = (bf16[256,512]{0,1:T(8,128)(2,1)}, bf16[256,512]{0,1:T(8,128)(2,1)S(1)}, u32[]{:S(2)}, u32[]{:S(2)}) collective-permute-start(bf16[256,512]{0,1:T(8,128)(2,1)} %copy.360), channel_id=1, source_target_pairs={{0,16},{2,18},{4,20},{6,22},{8,24},{10,26},{12,28},{14,30},{16,32}... | collective-permute-start | bytes 786440 | tf_op jit(solution)/shard_map/ppermute | solution.py:33
  129.4 22.7 %copy-start.16 = (bf16[256,512]{0,1:T(8,128)(2,1)}, bf16[256,512]{0,1:T(8,128)(2,1)S(1)}, u32[]{:S(2)}) copy-start(bf16[256,512]{0,1:T(8,128)(2,1)S(1)} %collective-permute-done.6) | copy-start | bytes 786436
  149.7 2.3 copy-start.20
  150.5 1.6 copy-start.18
  273.6 2.4 copy-start.12
  283.4 112.3 %collective-permute-start.10 = (bf16[256,512]{1,0:T(8,128)(2,1)}, bf16[256,512]{1,0:T(8,128)(2,1)}, u32[]{:S(2)}, u32[]{:S(2)}) collective-permute-start(bf16[256,512]{1,0:T(8,128)(2,1)} %pad_maximum_fusion.2), channel_id=1, source_target_pairs={{2,0},{4,2},{6,4},{8,6},{10,8},{12,10},{14,12},{16,14},{18,16},{20... | collective-permute-start | bytes 786440 | tf_op jit(solution)/shard_map/ppermute | solution.py:33
  293.7 106.6 %collective-permute-start.11 = (bf16[256,512]{1,0:T(8,128)(2,1)}, bf16[256,512]{1,0:T(8,128)(2,1)}, u32[]{:S(2)}, u32[]{:S(2)}) collective-permute-start(bf16[256,512]{1,0:T(8,128)(2,1)} %pad_maximum_fusion.3), channel_id=1, source_target_pairs={{4,0},{6,2},{8,4},{10,6},{12,8},{14,10},{16,12},{18,14},{20,16},{2... | collective-permute-start | bytes 786440 | tf_op jit(solution)/shard_map/ppermute | solution.py:33
  301.7 1.0 copy-start.1
  305.6 14.2 %copy-start.39 = (pred[256,256]{0,1:T(8,128)(4,1)S(1)}, pred[256,256]{0,1:T(8,128)(4,1)}, u32[]{:S(2)}) copy-start(pred[256,256]{0,1:T(8,128)(4,1)} %copy.199) | copy-start | bytes 196612
  305.6 96.6 %collective-permute-start.12 = (bf16[256,512]{1,0:T(8,128)(2,1)}, bf16[256,512]{1,0:T(8,128)(2,1)}, u32[]{:S(2)}, u32[]{:S(2)}) collective-permute-start(bf16[256,512]{1,0:T(8,128)(2,1)} %pad_maximum_fusion.4), channel_id=1, source_target_pairs={{6,0},{8,2},{10,4},{12,6},{14,8},{16,10},{18,12},{20,14},{22,16},{... | collective-permute-start | bytes 786440 | tf_op jit(solution)/shard_map/ppermute | solution.py:33
  322.0 1.0 copy-start.2
  324.2 8.6 %copy-start.17 = (bf16[256,512]{0,1:T(8,128)(2,1)S(1)}, bf16[256,512]{0,1:T(8,128)(2,1)}, u32[]{:S(2)}) copy-start(bf16[256,512]{0,1:T(8,128)(2,1)} %copy-done.16) | copy-start | bytes 786436
  326.0 80.8 %collective-permute-start.13 = (bf16[256,512]{1,0:T(8,128)(2,1)}, bf16[256,512]{1,0:T(8,128)(2,1)}, u32[]{:S(2)}, u32[]{:S(2)}) collective-permute-start(bf16[256,512]{1,0:T(8,128)(2,1)} %pad_maximum_fusion.5), channel_id=1, source_target_pairs={{8,0},{10,2},{12,4},{14,6},{16,8},{18,10},{20,12},{22,14},{24,16},... | collective-permute-start | bytes 786440 | tf_op jit(solution)/shard_map/ppermute | solution.py:33
  335.7 1.0 copy-start.4
  338.0 14.4 %copy-start.21 = (bf16[256,512]{0,1:T(8,128)(2,1)S(1)}, bf16[256,512]{0,1:T(8,128)(2,1)}, u32[]{:S(2)}) copy-start(bf16[256,512]{0,1:T(8,128)(2,1)} %copy-done.20) | copy-start | bytes 786436
  339.7 67.0 %collective-permute-start.14 = (bf16[256,512]{1,0:T(8,128)(2,1)}, bf16[256,512]{1,0:T(8,128)(2,1)}, u32[]{:S(2)}, u32[]{:S(2)}) collective-permute-start(bf16[256,512]{1,0:T(8,128)(2,1)} %pad_maximum_fusion.6), channel_id=1, source_target_pairs={{10,0},{12,2},{14,4},{16,6},{18,8},{20,10},{22,12},{24,14},{26,16}... | collective-permute-start | bytes 786440 | tf_op jit(solution)/shard_map/ppermute | solution.py:33
  355.3 1.0 copy-start.6
  357.4 6.1 %copy-start.19 = (bf16[256,512]{0,1:T(8,128)(2,1)S(1)}, bf16[256,512]{0,1:T(8,128)(2,1)}, u32[]{:S(2)}) copy-start(bf16[256,512]{0,1:T(8,128)(2,1)} %copy-done.18) | copy-start | bytes 786436
  366.5 1.1 copy-start.10
  368.7 6.1 %copy-start.15 = (bf16[256,512]{0,1:T(8,128)(2,1)S(1)}, bf16[256,512]{0,1:T(8,128)(2,1)}, u32[]{:S(2)}) copy-start(bf16[256,512]{0,1:T(8,128)(2,1)} %copy-done.14) | copy-start | bytes 786436
  377.7 1.0 copy-start.8
  379.2 3.6 copy-start.37
  380.0 2.8 copy-start.38
  385.1 1.0 copy-start
  385.1 2.2 copy-start.22
  386.1 2.9 copy-start.25
  387.3 3.3 copy-start.3
  387.3 3.3 copy-start.26
  389.0 2.0 copy-start.5
  389.0 2.0 copy-start.27
  390.7 1.2 copy-start.7
  390.7 1.2 copy-start.28
  391.0 1.3 copy-start.11
  391.0 1.3 copy-start.30
  391.9 1.0 copy-start.31
  391.9 1.0 copy-start.32
  391.9 1.7 copy-start.33
  391.9 1.7 copy-start.34
  392.2 2.1 copy-start.35
  392.2 2.1 copy-start.36
  392.2 2.8 copy-start.24
  393.6 1.8 copy-start.9
  393.6 1.8 copy-start.29
  395.8 26.4 %collective-permute-start.15 = (bf16[256,512]{1,0:T(8,128)(2,1)}, bf16[256,512]{1,0:T(8,128)(2,1)S(1)}, u32[]{:S(2)}, u32[]{:S(2)}) collective-permute-start(bf16[256,512]{1,0:T(8,128)(2,1)} %pad_maximum_fusion.7), channel_id=1, source_target_pairs={{12,0},{14,2},{16,4},{18,6},{20,8},{22,10},{24,12},{26,14},{28,16}... | collective-permute-start | bytes 786440 | tf_op jit(solution)/shard_map/ppermute | solution.py:33
  400.3 28.3 %collective-permute-start.16 = (bf16[256,512]{1,0:T(8,128)(2,1)}, bf16[256,512]{1,0:T(8,128)(2,1)S(1)}, u32[]{:S(2)}, u32[]{:S(2)}) collective-permute-start(bf16[256,512]{1,0:T(8,128)(2,1)} %pad_maximum_fusion.8), channel_id=1, source_target_pairs={{14,0},{16,2},{18,4},{20,6},{22,8},{24,10},{26,12},{28,14},{30,16}... | collective-permute-start | bytes 786440 | tf_op jit(solution)/shard_map/ppermute | solution.py:33
  402.2 31.7 %collective-permute-start.17 = (bf16[256,512]{1,0:T(8,128)(2,1)}, bf16[256,512]{1,0:T(8,128)(2,1)S(1)}, u32[]{:S(2)}, u32[]{:S(2)}) collective-permute-start(bf16[256,512]{1,0:T(8,128)(2,1)} %pad_maximum_fusion.9), channel_id=1, source_target_pairs={{16,0},{18,2},{20,4},{22,6},{24,8},{26,10},{28,12},{30,14},{32,16}... | collective-permute-start | bytes 786440 | tf_op jit(solution)/shard_map/ppermute | solution.py:33
  404.2 1.6 copy-start.13
  (1 other events, 0.8 us)
where the time goes:
time: 441 us; the launch traced here: 437 us
  local copies, waits for them, and re-layouts  136 us (31%)
  starting transfers between devices  97.4 us (22%)
  matrix products  95.5 us (22%)
  waiting for transfers between devices  69.7 us (16%)
  other arithmetic  36.6 us (8%)
    ppermute x16, starting transfers between devices, passed_along(): return lax.ppermute(block, axis, route)  75.7 us
    ppermute x16, waiting for transfers between devices, passed_along(): return lax.ppermute(block, axis, route)  46.8 us
    dynamic_slice x18, local copies, waits for them, and re-layouts, per_device(): lax.scan(second_pass, out_start, (stacked, visible_all, scores_all))  44.8 us
    dot_general x9, matrix products, second_pass(): jnp.einsum('gqtu,ugd->tgqd', probability_lowered, local_values, preferred...  23.9 us
    dot_general x9, matrix products, gradients(): jnp.einsum('nzev,enzx->vnx', probability_lowered, grad_four, preferred_el...  22.9 us
    unnamed x103, local copies, waits for them, and re-layouts  22.8 us
    dot_general x9, matrix products, gradients(): jnp.einsum('tgqd,ugd->gqtu', grad_four, local_values, preferred_element_t...  20.3 us
    squeeze x18, local copies, waits for them, and re-layouts, per_device(): unused_one, scores_all = lax.scan(score_pass, 0, (stacked, visible_all))  17.5 us
  transfers between devices with their start and end apart: 22, of which 10 were waited for; matrix products, arithmetic and copies ran while one was open for 26% of the time, Pallas kernels for 0%

commit v1 on v0

v1 whole, which is shorter than its diff:
```python
import math

import jax
import jax.numpy as jnp
from jax import lax
from jax.experimental import pallas as pl
from jax.experimental.pallas import tpu as pltpu
from jax.sharding import PartitionSpec as P

BLK = 128
HEAD = 128
TOK = 256
QH = 8
KVH = 2
PER = 4
QW = QH * HEAD
KW = KVH * HEAD
NSEQ = 128
ND = 9
WIDE = PER * TOK
SCALE = 1.0 / math.sqrt(HEAD)
C2 = SCALE * math.log2(math.e)
LOW = -1e30
MESH = pl.DeviceIdType.MESH
F32 = jnp.float32
BF16 = jnp.bfloat16


def dot(a, b):
    return lax.dot_general(a, b, (((1,), (0,)), ((), ())), preferred_element_type=F32)


def dot_nt(a, b):
    return lax.dot_general(a, b, (((1,), (1,)), ((), ())), preferred_element_type=F32)


def flip(a):
    return jnp.transpose(a, (1, 0))


def kernel(
    doc_ref,
    home_ref,
    q_in,
    k_in,
    v_in,
    g_in,
    att_ref,
    dq_ref,
    dk_ref,
    dv_ref,
    rq,
    rk,
    rv,
    rg,
    kv,
    kvt,
    qs,
    gs,
    gst,
    s_buf,
    p_buf,
    ds_buf,
    mx,
    lsum,
    delta,
    ot,
    attt,
    dqt,
    acc,
    sb,
    rr4,
    rr3,
    rr2,
    rr1,
    own_send,
    own_recv,
    halo_send,
    halo_recv,
    back_send,
    back_recv,
):
    s = lax.axis_index("seq")
    h = lax.axis_index("head")
    core = lax.rem(s, 2)
    xhi = lax.rem(lax.div(s, 2), 2)
    first = s == 0
    last = s == NSEQ - 1
    up4 = lax.rem(s + 4, NSEQ)
    down4 = lax.rem(s + NSEQ - 4, NSEQ)
    part_x = s + 2 - 4 * xhi
    part_c = s + 1 - 2 * core
    right = jnp.minimum(s + 1, NSEQ - 1)
    left = jnp.maximum(s - 1, 0)

    barrier = pltpu.get_barrier_semaphore()

    def greet(seq, head):
        pl.semaphore_signal(barrier, inc=1, device_id=(seq, head), device_id_type=MESH)

    for side in (left, right):
        greet(side, 1 - h)

        @pl.when(side != s)
        def _():
            greet(side, h)

    for other in (up4, down4, part_x):
        greet(other, h)
    edge = jnp.where(first | last, 1, 0)
    pl.semaphore_wait(barrier, 7 - edge)

    ins = (k_in, v_in, q_in, g_in)
    slots = (rk, rv, rq, rg)
    widths = (KW, KW, QW, QW)

    def direct(arrays, what):
        for side, seq in ((0, right), (1, left)):
            at_end = last if side == 0 else first
            base = jnp.where(at_end, 2 * (1 - side), 2 * side)
            slot = base + h
            for head in range(2):
                mine = at_end & (h == head)
                for a in arrays:
                    src = ins[a].at[:, pl.ds(head * widths[a], widths[a])]
                    copy = pltpu.make_async_remote_copy(
                        src_ref=src,
                        dst_ref=slots[a].at[slot],
                        send_sem=own_send.at[a, side, head],
                        recv_sem=own_recv.at[a, slot],
                        device_id=(seq, head),
                        device_id_type=MESH,
                    )
                    local = pltpu.make_async_copy(src, slots[a].at[slot], own_recv.at[a, slot])

                    if what == "start":

                        @pl.when(jnp.logical_not(mine))
                        def _():
                            copy.start()

                        @pl.when(mine)
                        def _():
                            local.start()

                    else:

                        @pl.when(jnp.logical_not(mine))
                        def _():
                            copy.wait_send()

    def landed(arrays):
        for a in arrays:
            for i in range(4):
                pltpu.make_async_copy(
                    slots[a].at[i], slots[a].at[i], own_recv.at[a, i]
                ).wait()

    direct((0, 1), "start")

    picks = []
    for p in range(2):
        wanted = 2 * s + p
        pick = jnp.int32(0)
        for i in range(4):
            shard = left if i < 2 else right
            pick = jnp.where(home_ref[2 * shard + i % 2] == wanted, i, pick)
        picks.append(pick)

    acc[...] = jnp.zeros_like(acc)
    ot[...] = jnp.zeros_like(ot)
    dqt[...] = jnp.zeros_like(dqt)
    mx[...] = jnp.full_like(mx, LOW)

    landed((0, 1))
    for p in range(2):
        for g in range(KVH):
            rows = pl.ds(p * BLK, BLK)
            cols = pl.ds(g * HEAD, HEAD)
            kv[0, g, rows, :] = rk[picks[p], :, cols]
            kv[0, KVH + g, rows, :] = rv[picks[p], :, cols]

    def halo(src, dst, seq, sem):
        return pltpu.make_async_remote_copy(
            src_ref=kv.at[src],
            dst_ref=kv.at[dst],
            send_sem=halo_send.at[sem],
            recv_sem=halo_recv.at[dst],
            device_id=(seq, h),
            device_id_type=MESH,
        )

    def have(d):
        pltpu.make_async_copy(kv.at[d], kv.at[d], halo_recv.at[d]).wait()

    z0 = halo(0, 4, up4, 0)
    z4 = halo(4, 8, up4, 1)
    x0 = halo(0, 2, part_x, 2)
    x4 = halo(4, 6 - 4 * xhi, part_x, 3)
    x8 = halo(8, 6, part_x, 4)
    c0 = halo(0, 1, part_c, 5)
    c2 = halo(2, 3 - 2 * core, part_c, 6)
    c4 = halo(4, 5 - 2 * core, part_c, 7)
    c6 = halo(6, 7 - 2 * core, part_c, 8)
    c8 = halo(8, 7, part_c, 9)

    z0.start()

    @pl.when(xhi == 0)
    def _():
        x0.start()

    @pl.when(core == 0)
    def _():
        c0.start()

    direct((2, 3), "start")

    have(4)
    z4.start()
    x4.start()
    c4.start()
    have(8)

    @pl.when(xhi == 1)
    def _():
        x8.start()

    @pl.when(core == 1)
    def _():
        c8.start()

    have(2)
    c2.start()
    have(6)
    c6.start()
    for d in (1, 3, 5, 7):
        have(d)

    def turn(d, carry):
        for i in range(2 * KVH):
            kvt[i, d] = flip(kv[d, i])
        return carry

    lax.fori_loop(0, ND, turn, 0)

    landed((2,))
    for p in range(2):
        for i in range(QH):
            rows = pl.ds((i % PER) * TOK + p * BLK, BLK)
            qs[i // PER, rows, :] = rq[picks[p], :, pl.ds(i * HEAD, HEAD)]

    lane = lax.broadcasted_iota(jnp.int32, (1, TOK), 1)

    def hidden(d, pu):
        back = s - d
        key_doc = doc_ref[jnp.maximum(2 * back + pu, 0)]
        low = []
        for pt in range(2):
            seen = (doc_ref[2 * s + pt] == key_doc) & (back >= 0)
            low.append(jnp.where(seen, 0.0, LOW).astype(F32))
        return jnp.where(lane < BLK, low[0], low[1])

    def score(d, g, shape):
        for j in range(PER):
            cols = pl.ds(j * TOK, TOK)
            tile = dot_nt(kv[d, g], qs[g, cols, :])
            if shape is not None:
                row = lax.broadcasted_iota(jnp.int32, (TOK, TOK), 0)
                col = lax.broadcasted_iota(jnp.int32, (TOK, TOK), 1)
                keep = row <= col if shape == "own" else row > col
                tile = jnp.where(keep, tile, LOW)
            s_buf[g * ND + d, :, cols] = tile
            best = mx[g, :, cols]
            for pu in range(2):
                top = jnp.max(tile[pu * BLK : (pu + 1) * BLK].reshape(BLK // 8, 8, TOK), axis=0)
                best = jnp.maximum(best, top + hidden(d, pu))
            mx[g, :, cols] = best

    for d, shape in ((0, "own"), (8, "far")):
        for g in range(KVH):
            score(d, g, shape)

    def score_step(i, carry):
        score(1 + lax.div(i, KVH), lax.rem(i, KVH), None)
        return carry

    lax.fori_loop(0, (ND - 2) * KVH, score_step, 0)

    def weigh(g, carry):
        lsum[...] = jnp.zeros_like(lsum)
        top = jnp.max(mx[g], axis=0, keepdims=True) * C2

        def step(d, inner):
            low = [hidden(d, pu) for pu in range(2)]
            for j in range(PER):
                cols = pl.ds(j * TOK, TOK)
                total = lsum[:, cols]
                for pu in range(2):
                    rows = pl.ds(pu * BLK, BLK)
                    base = top[:, j * TOK : (j + 1) * TOK] - low[pu]
                    e = jnp.exp2(s_buf[g * ND + d, rows, cols] * C2 - base)
                    total = total + jnp.sum(e.reshape(BLK // 8, 8, TOK), axis=0)
                    p_buf[g * ND + d, rows, cols] = e.astype(BF16)
                lsum[:, cols] = total
                ot[g, :, cols] += dot(kvt[KVH + g, d], p_buf[g * ND + d, :, cols])
            return inner

        lax.fori_loop(0, ND, step, 0)
        inv = 1.0 / jnp.sum(lsum[...], axis=0, keepdims=True)
        attt[g] = (ot[g] * inv).astype(BF16)
        delta[g] = inv
        return carry

    lax.fori_loop(0, KVH, weigh, 0)

    landed((3,))
    for i in range(QH):
        g, j = i // PER, i % PER
        cols = pl.ds(j * TOK, TOK)
        for p in range(2):
            gs[g, pl.ds(j * TOK + p * BLK, BLK), :] = rg[picks[p], :, pl.ds(i * HEAD, HEAD)]
        low = (flip(gs[g, cols, :]).astype(F32) * delta[g, :, cols]).astype(BF16)
        gst[g, :, cols] = low
        gs[g, cols, :] = flip(low)
        a = attt[g, :, cols]
        delta[g, :, cols] = jnp.sum(low.astype(F32) * a.astype(F32), axis=0, keepdims=True)
        att_ref[:, pl.ds(i * HEAD, HEAD)] = flip(a)

    def slope(d):
        def one(g, carry):
            for j in range(PER):
                cols = pl.ds(j * TOK, TOK)
                dp = dot(kv[d, KVH + g], gst[g, :, cols])
                e = p_buf[g * ND + d, :, cols].astype(F32)
                ds_buf[:, cols] = (e * (dp - delta[g, :, cols])).astype(BF16)
                dqt[g, :, cols] += dot(kvt[g, d], ds_buf[:, cols])
            acc[d, g] += dot(ds_buf[...], qs[g])
            acc[d, KVH + g] += dot(p_buf[g * ND + d], gs[g])
            return carry

        lax.fori_loop(0, KVH, one, 0)

    def give(d, dst, seq, sem):
        return pltpu.make_async_remote_copy(
            src_ref=sb.at[d],
            dst_ref=dst,
            send_sem=back_send.at[sem],
            recv_sem=back_recv.at[sem],
            device_id=(seq, h),
            device_id_type=MESH,
        )

    b7 = give(7, rr4.at[3], part_c, 3)
    b5 = give(5, rr4.at[2], part_c, 2)
    b3 = give(3, rr4.at[1], part_c, 1)
    b1 = give(1, rr4.at[0], part_c, 0)
    b6 = give(6, rr3.at[1], part_x, 5)
    b2 = give(2, rr3.at[0], part_x, 4)
    b8 = give(8, rr2, down4, 6)
    b4 = give(4, rr1, down4, 7)

    def post(d, copy):
        sb[d] = acc[d].astype(BF16)
        copy.start()

    def take(copy, ref, d):
        copy.wait_recv()
        acc[d] += ref[...].astype(F32)

    slope(7)
    post(7, b7)
    slope(5)
    post(5, b5)
    slope(6)
    take(b7, rr4.at[3], 6 + 2 * core)
    take(b5, rr4.at[2], 4 + 2 * core)
    post(6, b6)
    slope(3)
    post(3, b3)
    slope(1)
    post(1, b1)
    slope(8)
    take(b6, rr3.at[1], 4 + 4 * xhi)
    post(8, b8)
    slope(2)
    take(b3, rr4.at[1], 2 + 2 * core)
    take(b1, rr4.at[0], 2 * core)
    post(2, b2)
    slope(4)
    take(b2, rr3.at[0], 4 * xhi)
    take(b8, rr2, 4)
    post(4, b4)
    slope(0)
    for i in range(QH):
        g, j = i // PER, i % PER
        low = (dqt[g, :, pl.ds(j * TOK, TOK)] * SCALE).astype(BF16)
        dq_ref[:, pl.ds(i * HEAD, HEAD)] = flip(low)
    take(b4, rr1, 0)
    for g in range(KVH):
        dk_ref[:, pl.ds(g * HEAD, HEAD)] = (acc[0, g] * SCALE).astype(BF16)
        dv_ref[:, pl.ds(g * HEAD, HEAD)] = acc[0, KVH + g].astype(BF16)

    direct((0, 1, 2, 3), "wait")
    for copy in (z0, z4, x4, c2, c4, c6, b7, b5, b3, b1, b6, b2, b8, b4):
        copy.wait_send()

    @pl.when(xhi == 0)
    def _():
        x0.wait_send()

    @pl.when(xhi == 1)
    def _():
        x8.wait_send()

    @pl.when(core == 0)
    def _():
        c0.wait_send()

    @pl.when(core == 1)
    def _():
        c8.wait_send()


def per_device(queries, key_states, value_vector_rows, grad_output, doc_ids, block_home):
    vmem = pl.BlockSpec(memory_space=pltpu.VMEM)
    smem = pl.BlockSpec(memory_space=pltpu.SMEM)
    anywhere = pl.BlockSpec(memory_space=pl.ANY)
    out = pl.pallas_call(
        kernel,
        out_shape=(
            jax.ShapeDtypeStruct((TOK, QW), BF16),
            jax.ShapeDtypeStruct((TOK, QW), BF16),
            jax.ShapeDtypeStruct((TOK, KW), BF16),
            jax.ShapeDtypeStruct((TOK, KW), BF16),
        ),
        in_specs=[smem, smem, anywhere, anywhere, anywhere, anywhere],
        out_specs=(vmem, vmem, vmem, vmem),
        scratch_shapes=[
            pltpu.VMEM((4, BLK, QW), BF16),
            pltpu.VMEM((4, BLK, KW), BF16),
            pltpu.VMEM((4, BLK, KW), BF16),
            pltpu.VMEM((4, BLK, QW), BF16),
            pltpu.VMEM((ND, 2 * KVH, TOK, HEAD), BF16),
            pltpu.VMEM((2 * KVH, ND, HEAD, TOK), BF16),
            pltpu.VMEM((KVH, WIDE, HEAD), BF16),
            pltpu.VMEM((KVH, WIDE, HEAD), BF16),
            pltpu.VMEM((KVH, HEAD, WIDE), BF16),
            pltpu.VMEM((KVH * ND, TOK, WIDE), F32),
            pltpu.VMEM((KVH * ND, TOK, WIDE), BF16),
            pltpu.VMEM((TOK, WIDE), BF16),
            pltpu.VMEM((KVH, 8, WIDE), F32),
            pltpu.VMEM((8, WIDE), F32),
            pltpu.VMEM((KVH, 1, WIDE), F32),
            pltpu.VMEM((KVH, HEAD, WIDE), F32),
            pltpu.VMEM((KVH, HEAD, WIDE), BF16),
            pltpu.VMEM((KVH, HEAD, WIDE), F32),
            pltpu.VMEM((ND, 2 * KVH, TOK, HEAD), F32),
            pltpu.VMEM((ND, 2 * KVH, TOK, HEAD), BF16),
            pltpu.VMEM((4, 2 * KVH, TOK, HEAD), BF16),
            pltpu.VMEM((2, 2 * KVH, TOK, HEAD), BF16),
            pltpu.VMEM((2 * KVH, TOK, HEAD), BF16),
            pltpu.VMEM((2 * KVH, TOK, HEAD), BF16),
            pltpu.SemaphoreType.DMA((4, 2, 2)),
            pltpu.SemaphoreType.DMA((4, 4)),
            pltpu.SemaphoreType.DMA((10,)),
            pltpu.SemaphoreType.DMA((ND,)),
            pltpu.SemaphoreType.DMA((8,)),
            pltpu.SemaphoreType.DMA((8,)),
        ],
        compiler_params=pltpu.CompilerParams(
            collective_id=0,
            has_side_effects=True,
            vmem_limit_bytes=60 * 1024 * 1024,
        ),
        cost_estimate=pl.CostEstimate(
            flops=8 * 10**9, bytes_accessed=3 * 10**6, transcendentals=5 * 10**6
        ),
    )(doc_ids, block_home, queries, key_states, value_vector_rows, grad_output)
    return out


def solution(mesh):
    return jax.shard_map(
        per_device,
        mesh=mesh,
        in_specs=(
            P(("seq", "head"), None),
            P(("seq", "head"), None),
            P(("seq", "head"), None),
            P(("seq", "head"), None),
            P(),
            P(),
        ),
        out_specs=(P("seq", "head"), P("seq", "head"), P("seq", "head"), P("seq", "head")),
        check_vma=False,
    )
```

time: 441 us -> 121 us (0.27)
  the two profiles are of different devices: /device:TPU:40 before, /device:TPU:1 now
where the time goes in v1:
time: 121 us
  Pallas kernels  115 us (95%)
  local copies, waits for them, and re-layouts  4.56 us (4%)
    pallas_call x1, Pallas kernels, per_device(): pl.pallas_call(kernel, out_shape=(jax.ShapeDtypeStruct((TOK, QW), BF16),...  115 us
    unnamed x10, local copies, waits for them, and re-layouts  4.56 us

profile of v1, /device:TPU:1, one launch (start us, length us, event | category | flops | bytes accessed | tf_op | source)
XLA Modules:
  0.0 120.7 jit_solution(14644304817313140380)
XLA Ops:
  0.6 115.5 %shard_map.93 = (bf16[256,1024]{1,0:T(8,128)(2,1)}, bf16[256,1024]{1,0:T(8,128)(2,1)}, bf16[256,256]{1,0:T(8,128)(2,1)}, bf16[256,256]{1,0:T(8,128)(2,1)}) custom-call(s32[256]{0:T(256)} %doc_ref.1, s32[256]{0:T(256)} %home_ref.1, bf16[128,2048]{1,0:T(8,128)(2,1)} %q_in.1, bf16[128,512]{1,0:T(8,128)(2,1)} %k_in.1, bf16[128,512]{1,0:T(8,128)(2,1)} %v_in.1, ...), custom_call_target="tpu_custom_call" | custom-call | flops 8000000000 | bytes 3000000 | tf_op jit(solution)/shard_map/pallas_call | solution.py:429
  116.1 0.0 copy-start
  116.1 1.9 %copy.14 = bf16[256,1024]{1,0:T(8,128)(2,1)} copy(bf16[256,1024]{1,0:T(8,128)(2,1)} %get-tuple-element.8) | data formatting | bytes 1048576
  118.0 0.0 copy-done
  118.0 0.0 copy-start.2
  118.0 0.8 copy.15
  118.8 0.2 copy-done.2
  119.1 0.0 copy-start.1
  119.1 0.7 copy.16
  119.7 0.3 copy-done.1
  120.0 0.7 copy.17
Async XLA Ops:
  116.1 1.9 %copy-start = (bf16[256,1024]{1,0:T(8,128)(2,1)S(1)}, bf16[256,1024]{1,0:T(8,128)(2,1)}, u32[]{:S(2)}) copy-start(bf16[256,1024]{1,0:T(8,128)(2,1)} %get-tuple-element.9) | copy-start | bytes 1572868
  118.0 1.0 copy-start.2
  119.1 1.0 copy-start.1

commit v2 on v1

v2 whole, which is shorter than its diff:
```python
import math

import jax
import jax.numpy as jnp
from jax import lax
from jax.experimental import pallas as pl
from jax.experimental.pallas import tpu as pltpu
from jax.sharding import PartitionSpec as P

BLK = 128
HEAD = 128
TOK = 256
QH = 8
KVH = 2
PER = 4
QW = QH * HEAD
KW = KVH * HEAD
NSEQ = 128
ND = 9
WIDE = PER * TOK
SCALE = 1.0 / math.sqrt(HEAD)
C2 = SCALE * math.log2(math.e)
LOW = -1e30
MESH = pl.DeviceIdType.MESH
F32 = jnp.float32
BF16 = jnp.bfloat16


def dot(a, b):
    return lax.dot_general(a, b, (((1,), (0,)), ((), ())), preferred_element_type=F32)


def dot_nt(a, b):
    return lax.dot_general(a, b, (((1,), (1,)), ((), ())), preferred_element_type=F32)


def flip(a):
    return jnp.transpose(a, (1, 0))


def kernel(
    doc_ref,
    home_ref,
    q_in,
    k_in,
    v_in,
    g_in,
    att_ref,
    dq_ref,
    dk_ref,
    dv_ref,
    loc_q,
    loc_k,
    loc_v,
    loc_g,
    m_out,
    m_got,
    x_out,
    x_got,
    c_out,
    c_got,
    kv,
    kvt,
    qs,
    gs,
    gst,
    s_buf,
    p_buf,
    ds_buf,
    mx,
    lsum,
    delta,
    ot,
    attt,
    dqt,
    acc,
    sb,
    rr4,
    rr3,
    rr2,
    rr1,
    load_sem,
    move_send,
    move_recv,
    halo_send,
    halo_recv,
    back_send,
    back_recv,
):
    s = lax.axis_index("seq")
    h = lax.axis_index("head")
    core = lax.rem(s, 2)
    xhi = lax.rem(lax.div(s, 2), 2)
    up4 = lax.rem(s + 4, NSEQ)
    down4 = lax.rem(s + NSEQ - 4, NSEQ)
    part_x = s + 2 - 4 * xhi
    part_c = s + 1 - 2 * core
    cross = jnp.clip(s - 1 + 2 * core, 0, NSEQ - 1)

    ins = (k_in, v_in, q_in, g_in)
    locs = (loc_k, loc_v, loc_q, loc_g)
    widths = (KW, KW, QW, QW)

    def load(a, half):
        return pltpu.make_async_copy(
            ins[a].at[:, pl.ds(half * widths[a], widths[a])],
            locs[a].at[half],
            load_sem.at[a, half],
        )

    for a in range(4):
        for half in range(2):
            load(a, half).start()

    barrier = pltpu.get_barrier_semaphore()

    def greet(seq, head):
        pl.semaphore_signal(barrier, inc=1, device_id=(seq, head), device_id_type=MESH)

    greet(s, 1 - h)
    greet(cross, 1 - h)
    for other in (part_c, part_x, up4, down4):
        greet(other, h)
    pl.semaphore_wait(barrier, 6)

    crosses = lax.div(home_ref[2 * s + h], 2) != part_c
    told = jnp.where(crosses, h, 1 - h)

    def column(i):
        if i < 2 * KVH:
            return i % 2, i // 2
        i -= 2 * KVH
        return 2 + i // QH, i % QH

    pieces = ((0, 2), (2, 4), (4, 8), (8, 12), (12, 16), (16, 20))

    def own(i, half):
        a, c = column(i)
        return locs[a][half, :, pl.ds(c * HEAD, HEAD)]

    def move(way, piece):
        lo, hi = pieces[piece]
        src, dst, to = (
            (m_out, m_got, (s, 1 - h)),
            (x_out, x_got, (cross, 1 - h)),
            (c_out, c_got, (part_c, h)),
        )[way]
        return pltpu.make_async_remote_copy(
            src_ref=src.at[pl.ds(lo, hi - lo)],
            dst_ref=dst.at[pl.ds(lo, hi - lo)],
            send_sem=move_send.at[way, piece],
            recv_sem=move_recv.at[way, piece],
            device_id=to,
            device_id_type=MESH,
        )

    def tell(piece):
        for i in range(*pieces[piece]):
            m_out[i] = own(i, told)
        move(0, piece).start()

    def pass_on(piece):
        move(0, piece).wait_recv()
        for i in range(*pieces[piece]):
            got = m_got[i]
            x_out[i] = lax.select(crosses, own(i, 1 - h), got)
            c_out[i] = lax.select(crosses, got, own(i, h))
        move(1, piece).start()
        move(2, piece).start()

    inside = []
    for p in range(2):
        want = 2 * s + p
        inside.append((home_ref[2 * part_c] == want) | (home_ref[2 * part_c + 1] == want))

    def settle(piece):
        move(1, piece).wait_recv()
        move(2, piece).wait_recv()
        for i in range(*pieces[piece]):
            a, c = column(i)
            for p in range(2):
                block = lax.select(inside[p], c_got[i], x_got[i])
                if a < 2:
                    kv[0, c, a, pl.ds(p * BLK, BLK), :] = block
                else:
                    rows = pl.ds((c % PER) * TOK + p * BLK, BLK)
                    (qs if a == 2 else gs)[c // PER, rows, :] = block

    def halo(src, dst, seq, sem, g):
        return pltpu.make_async_remote_copy(
            src_ref=kv.at[src, g],
            dst_ref=kv.at[dst, g],
            send_sem=halo_send.at[sem, g],
            recv_sem=halo_recv.at[dst, g],
            device_id=(seq, h),
            device_id_type=MESH,
        )

    def have(d, g):
        pltpu.make_async_copy(kv.at[d, g], kv.at[d, g], halo_recv.at[d, g]).wait()

    z0, z4, x0, x4, x8, c0, c2, c4, c6, c8 = (
        [halo(src, dst, seq, sem, g) for g in range(KVH)]
        for sem, (src, dst, seq) in enumerate(
            (
                (0, 4, up4),
                (4, 8, up4),
                (0, 2, part_x),
                (4, 6 - 4 * xhi, part_x),
                (8, 6, part_x),
                (0, 1, part_c),
                (2, 3 - 2 * core, part_c),
                (4, 5 - 2 * core, part_c),
                (6, 7 - 2 * core, part_c),
                (8, 7, part_c),
            )
        )
    )

    for a in (0, 1):
        for half in range(2):
            load(a, half).wait()
    tell(0)
    tell(1)
    acc[...] = jnp.zeros_like(acc)
    pass_on(0)
    pass_on(1)
    for a in (2, 3):
        for half in range(2):
            load(a, half).wait()
    tell(2)
    tell(3)
    ot[...] = jnp.zeros_like(ot)
    dqt[...] = jnp.zeros_like(dqt)
    mx[...] = jnp.full_like(mx, LOW)
    for g in range(KVH):
        settle(g)
        z0[g].start()

        @pl.when(xhi == 0)
        def _():
            x0[g].start()

        @pl.when(core == 0)
        def _():
            c0[g].start()

    tell(4)
    tell(5)
    pass_on(2)
    pass_on(3)
    for g in range(KVH):
        have(4, g)
        z4[g].start()
        x4[g].start()
        c4[g].start()
    pass_on(4)
    pass_on(5)
    for g in range(KVH):
        have(8, g)

        @pl.when(xhi == 1)
        def _():
            x8[g].start()

        @pl.when(core == 1)
        def _():
            c8[g].start()

    for d, copy in ((2, c2), (6, c6)):
        for g in range(KVH):
            have(d, g)
            copy[g].start()
    for d in (1, 3, 5, 7):
        for g in range(KVH):
            have(d, g)

    def turn(d, carry):
        for g in range(KVH):
            for kind in range(2):
                kvt[kind * KVH + g, d] = flip(kv[d, g, kind])
        return carry

    lax.fori_loop(0, ND, turn, 0)

    settle(2)
    settle(3)

    lane = lax.broadcasted_iota(jnp.int32, (1, TOK), 1)

    def hidden(d, pu):
        back = s - d
        key_doc = doc_ref[jnp.maximum(2 * back + pu, 0)]
        low = []
        for pt in range(2):
            seen = (doc_ref[2 * s + pt] == key_doc) & (back >= 0)
            low.append(jnp.where(seen, 0.0, LOW).astype(F32))
        return jnp.where(lane < BLK, low[0], low[1])

    def score(d, g, shape):
        for j in range(PER):
            cols = pl.ds(j * TOK, TOK)
            tile = dot_nt(kv[d, g, 0], qs[g, cols, :])
            if shape is not None:
                row = lax.broadcasted_iota(jnp.int32, (TOK, TOK), 0)
                col = lax.broadcasted_iota(jnp.int32, (TOK, TOK), 1)
                keep = row <= col if shape == "own" else row > col
                tile = jnp.where(keep, tile, LOW)
            s_buf[g * ND + d, :, cols] = tile
            best = mx[g, :, cols]
            for pu in range(2):
                top = jnp.max(tile[pu * BLK : (pu + 1) * BLK].reshape(BLK // 8, 8, TOK), axis=0)
                best = jnp.maximum(best, top + hidden(d, pu))
            mx[g, :, cols] = best

    for d, shape in ((0, "own"), (8, "far")):
        for g in range(KVH):
            score(d, g, shape)

    def score_step(i, carry):
        score(1 + lax.div(i, KVH), lax.rem(i, KVH), None)
        return carry

    lax.fori_loop(0, (ND - 2) * KVH, score_step, 0)

    def weigh(g, carry):
        lsum[...] = jnp.zeros_like(lsum)
        top = jnp.max(mx[g], axis=0, keepdims=True) * C2

        def step(d, inner):
            low = [hidden(d, pu) for pu in range(2)]
            for j in range(PER):
                cols = pl.ds(j * TOK, TOK)
                total = lsum[:, cols]
                for pu in range(2):
                    rows = pl.ds(pu * BLK, BLK)
                    base = top[:, j * TOK : (j + 1) * TOK] - low[pu]
                    e = jnp.exp2(s_buf[g * ND + d, rows, cols] * C2 - base)
                    total = total + jnp.sum(e.reshape(BLK // 8, 8, TOK), axis=0)
                    p_buf[g * ND + d, rows, cols] = e.astype(BF16)
                lsum[:, cols] = total
                ot[g, :, cols] += dot(kvt[KVH + g, d], p_buf[g * ND + d, :, cols])
            return inner

        lax.fori_loop(0, ND, step, 0)
        inv = 1.0 / jnp.sum(lsum[...], axis=0, keepdims=True)
        attt[g] = (ot[g] * inv).astype(BF16)
        delta[g] = inv
        return carry

    lax.fori_loop(0, KVH, weigh, 0)

    settle(4)
    settle(5)
    for i in range(QH):
        g, j = i // PER, i % PER
        cols = pl.ds(j * TOK, TOK)
        low = (flip(gs[g, cols, :]).astype(F32) * delta[g, :, cols]).astype(BF16)
        gst[g, :, cols] = low
        gs[g, cols, :] = flip(low)
        a = attt[g, :, cols]
        delta[g, :, cols] = jnp.sum(low.astype(F32) * a.astype(F32), axis=0, keepdims=True)
        att_ref[:, pl.ds(i * HEAD, HEAD)] = flip(a)

    def slope(d, g):
        for j in range(PER):
            cols = pl.ds(j * TOK, TOK)
            dp = dot(kv[d, g, 1], gst[g, :, cols])
            e = p_buf[g * ND + d, :, cols].astype(F32)
            ds_buf[:, cols] = (e * (dp - delta[g, :, cols])).astype(BF16)
            dqt[g, :, cols] += dot(kvt[g, d], ds_buf[:, cols])
        acc[d, g, 0] += dot(ds_buf[...], qs[g])
        acc[d, g, 1] += dot(p_buf[g * ND + d], gs[g])

    def give(d, dst, seq, sem):
        return [
            pltpu.make_async_remote_copy(
                src_ref=sb.at[d, g],
                dst_ref=dst.at[g],
                send_sem=back_send.at[sem, g],
                recv_sem=back_recv.at[sem, g],
                device_id=(seq, h),
                device_id_type=MESH,
            )
            for g in range(KVH)
        ]

    b7 = give(7, rr4.at[3], part_c, 3)
    b5 = give(5, rr4.at[2], part_c, 2)
    b3 = give(3, rr4.at[1], part_c, 1)
    b1 = give(1, rr4.at[0], part_c, 0)
    b6 = give(6, rr3.at[1], part_x, 5)
    b2 = give(2, rr3.at[0], part_x, 4)
    b8 = give(8, rr2, down4, 6)
    b4 = give(4, rr1, down4, 7)

    def post(d, copy, g):
        sb[d, g] = acc[d, g].astype(BF16)
        copy[g].start()

    def take(copy, ref, d, g):
        copy[g].wait_recv()
        acc[d, g] += ref[g].astype(F32)

    for g in range(KVH):
        slope(7, g)
        post(7, b7, g)
        slope(5, g)
        post(5, b5, g)
        slope(6, g)
        take(b7, rr4.at[3], 6 + 2 * core, g)
        take(b5, rr4.at[2], 4 + 2 * core, g)
        post(6, b6, g)
    for g in range(KVH):
        slope(3, g)
        post(3, b3, g)
        slope(1, g)
        post(1, b1, g)
        slope(2, g)
        take(b3, rr4.at[1], 2 + 2 * core, g)
        take(b1, rr4.at[0], 2 * core, g)
        post(2, b2, g)
        slope(8, g)
        take(b6, rr3.at[1], 4 + 4 * xhi, g)
        post(8, b8, g)
    for g in range(KVH):
        slope(4, g)
        slope(0, g)
        take(b2, rr3.at[0], 4 * xhi, g)
        take(b8, rr2, 4, g)
        post(4, b4, g)
    for i in range(QH):
        g, j = i // PER, i % PER
        low = (dqt[g, :, pl.ds(j * TOK, TOK)] * SCALE).astype(BF16)
        dq_ref[:, pl.ds(i * HEAD, HEAD)] = flip(low)
    for g in range(KVH):
        take(b4, rr1, 0, g)
        dk_ref[:, pl.ds(g * HEAD, HEAD)] = (acc[0, g, 0] * SCALE).astype(BF16)
        dv_ref[:, pl.ds(g * HEAD, HEAD)] = acc[0, g, 1].astype(BF16)

    for way in range(3):
        for piece in range(len(pieces)):
            move(way, piece).wait_send()
    for copy in (z0, z4, x4, c2, c4, c6, b7, b5, b3, b1, b6, b2, b8, b4):
        for g in range(KVH):
            copy[g].wait_send()

    for ahead, copy in ((xhi == 0, x0), (xhi == 1, x8), (core == 0, c0), (core == 1, c8)):

        @pl.when(ahead)
        def _():
            for g in range(KVH):
                copy[g].wait_send()


def per_device(queries, key_states, value_vector_rows, grad_output, doc_ids, block_home):
    vmem = pl.BlockSpec(memory_space=pltpu.VMEM)
    smem = pl.BlockSpec(memory_space=pltpu.SMEM)
    anywhere = pl.BlockSpec(memory_space=pl.ANY)
    out = pl.pallas_call(
        kernel,
        out_shape=(
            jax.ShapeDtypeStruct((TOK, QW), BF16),
            jax.ShapeDtypeStruct((TOK, QW), BF16),
            jax.ShapeDtypeStruct((TOK, KW), BF16),
            jax.ShapeDtypeStruct((TOK, KW), BF16),
        ),
        in_specs=[smem, smem, anywhere, anywhere, anywhere, anywhere],
        out_specs=(vmem, vmem, vmem, vmem),
        scratch_shapes=[
            pltpu.VMEM((2, BLK, QW), BF16),
            pltpu.VMEM((2, BLK, KW), BF16),
            pltpu.VMEM((2, BLK, KW), BF16),
            pltpu.VMEM((2, BLK, QW), BF16),
            *[pltpu.VMEM((2 * KVH + 2 * QH, BLK, HEAD), BF16) for _ in range(6)],
            pltpu.VMEM((ND, KVH, 2, TOK, HEAD), BF16),
            pltpu.VMEM((2 * KVH, ND, HEAD, TOK), BF16),
            pltpu.VMEM((KVH, WIDE, HEAD), BF16),
            pltpu.VMEM((KVH, WIDE, HEAD), BF16),
            pltpu.VMEM((KVH, HEAD, WIDE), BF16),
            pltpu.VMEM((KVH * ND, TOK, WIDE), F32),
            pltpu.VMEM((KVH * ND, TOK, WIDE), BF16),
            pltpu.VMEM((TOK, WIDE), BF16),
            pltpu.VMEM((KVH, 8, WIDE), F32),
            pltpu.VMEM((8, WIDE), F32),
            pltpu.VMEM((KVH, 1, WIDE), F32),
            pltpu.VMEM((KVH, HEAD, WIDE), F32),
            pltpu.VMEM((KVH, HEAD, WIDE), BF16),
            pltpu.VMEM((KVH, HEAD, WIDE), F32),
            pltpu.VMEM((ND, KVH, 2, TOK, HEAD), F32),
            pltpu.VMEM((ND, KVH, 2, TOK, HEAD), BF16),
            pltpu.VMEM((4, KVH, 2, TOK, HEAD), BF16),
            pltpu.VMEM((2, KVH, 2, TOK, HEAD), BF16),
            pltpu.VMEM((KVH, 2, TOK, HEAD), BF16),
            pltpu.VMEM((KVH, 2, TOK, HEAD), BF16),
            pltpu.SemaphoreType.DMA((4, 2)),
            pltpu.SemaphoreType.DMA((3, 6)),
            pltpu.SemaphoreType.DMA((3, 6)),
            pltpu.SemaphoreType.DMA((10, KVH)),
            pltpu.SemaphoreType.DMA((ND, KVH)),
            pltpu.SemaphoreType.DMA((8, KVH)),
            pltpu.SemaphoreType.DMA((8, KVH)),
        ],
        compiler_params=pltpu.CompilerParams(
            collective_id=0,
            has_side_effects=True,
            vmem_limit_bytes=60 * 1024 * 1024,
        ),
        cost_estimate=pl.CostEstimate(
            flops=8 * 10**9, bytes_accessed=3 * 10**6, transcendentals=5 * 10**6
        ),
    )(doc_ids, block_home, queries, key_states, value_vector_rows, grad_output)
    return out


def solution(mesh):
    return jax.shard_map(
        per_device,
        mesh=mesh,
        in_specs=(
            P(("seq", "head"), None),
            P(("seq", "head"), None),
            P(("seq", "head"), None),
            P(("seq", "head"), None),
            P(),
            P(),
        ),
        out_specs=(P("seq", "head"), P("seq", "head"), P("seq", "head"), P("seq", "head")),
        check_vma=False,
    )
```

time: 121 us -> 92.1 us (0.76)
  Pallas kernels: 115 us -> 86.7 us
    pallas_call x1, Pallas kernels: 115 us -> 86.7 us  [per_device(): pl.pallas_call(kernel, out_shape=(jax.ShapeDtypeStruct((TOK, QW), BF16),...]
where the time goes in v2:
time: 92.1 us; the launch traced here: 91.9 us
  Pallas kernels  86.7 us (94%)
  local copies, waits for them, and re-layouts  4.56 us (5%)
    pallas_call x1, Pallas kernels, per_device(): pl.pallas_call(kernel, out_shape=(jax.ShapeDtypeStruct((TOK, QW), BF16),...  86.7 us
    unnamed x10, local copies, waits for them, and re-layouts  4.56 us

profile of v2, /device:TPU:1, one launch (start us, length us, event | category | flops | bytes accessed | tf_op | source)
XLA Modules:
  0.0 91.9 jit_solution(5465859883816890179)
XLA Ops:
  0.6 86.7 %shard_map.93 = (bf16[256,1024]{1,0:T(8,128)(2,1)}, bf16[256,1024]{1,0:T(8,128)(2,1)}, bf16[256,256]{1,0:T(8,128)(2,1)}, bf16[256,256]{1,0:T(8,128)(2,1)}) custom-call(s32[256]{0:T(256)} %doc_ref.1, s32[256]{0:T(256)} %home_ref.1, bf16[128,2048]{1,0:T(8,128)(2,1)} %q_in.1, bf16[128,512]{1,0:T(8,128)(2,1)} %k_in.1, bf16[128,512]{1,0:T(8,128)(2,1)} %v_in.1, ...), custom_call_target="tpu_custom_call" | custom-call | flops 8000000000 | bytes 3000000 | tf_op jit(solution)/shard_map/pallas_call | solution.py:460
  87.4 0.0 copy-start
  87.4 1.9 %copy.14 = bf16[256,1024]{1,0:T(8,128)(2,1)} copy(bf16[256,1024]{1,0:T(8,128)(2,1)} %get-tuple-element.8) | data formatting | bytes 1048576
  89.3 0.0 copy-done
  89.3 0.0 copy-start.2
  89.3 0.8 copy.15
  90.1 0.2 copy-done.2
  90.3 0.0 copy-start.1
  90.3 0.7 copy.16
  91.0 0.3 copy-done.1
  91.3 0.7 copy.17
Async XLA Ops:
  87.4 1.9 %copy-start = (bf16[256,1024]{1,0:T(8,128)(2,1)S(1)}, bf16[256,1024]{1,0:T(8,128)(2,1)}, u32[]{:S(2)}) copy-start(bf16[256,1024]{1,0:T(8,128)(2,1)} %get-tuple-element.9) | copy-start | bytes 1572868
  89.3 1.0 %copy-start.2 = (bf16[256,256]{1,0:T(8,128)(2,1)S(1)}, bf16[256,256]{1,0:T(8,128)(2,1)}, u32[]{:S(2)}) copy-start(bf16[256,256]{1,0:T(8,128)(2,1)} %get-tuple-element.10) | copy-start | bytes 393220
  90.3 1.0 %copy-start.1 = (bf16[256,256]{1,0:T(8,128)(2,1)S(1)}, bf16[256,256]{1,0:T(8,128)(2,1)}, u32[]{:S(2)}) copy-start(bf16[256,256]{1,0:T(8,128)(2,1)} %get-tuple-element.11) | copy-start | bytes 393220

commit v3 on v2

v3 whole, which is shorter than its diff:
```python
import math

import jax
import jax.numpy as jnp
from jax import lax
from jax.experimental import pallas as pl
from jax.experimental.pallas import tpu as pltpu
from jax.sharding import PartitionSpec as P

BLK = 128
HEAD = 128
TOK = 256
QH = 8
KVH = 2
PER = 4
QW = QH * HEAD
KW = KVH * HEAD
NSEQ = 128
ND = 9
WIDE = PER * TOK
SCALE = 1.0 / math.sqrt(HEAD)
C2 = SCALE * math.log2(math.e)
LOW = -1e30
ORDER = (0, 8, 4, 2, 1, 3, 6, 5, 7)
PLACE = {d: i for i, d in enumerate(ORDER)}
EARLY = 6
MESH = pl.DeviceIdType.MESH
F32 = jnp.float32
BF16 = jnp.bfloat16


def dot(a, b):
    return lax.dot_general(a, b, (((1,), (0,)), ((), ())), preferred_element_type=F32)


def dot_nt(a, b):
    return lax.dot_general(a, b, (((1,), (1,)), ((), ())), preferred_element_type=F32)


def flip(a):
    return jnp.transpose(a, (1, 0))


def kernel(
    doc_ref,
    home_ref,
    q_in,
    k_in,
    v_in,
    g_in,
    att_out,
    dq_out,
    dk_out,
    dv_out,
    att_ref,
    dq_ref,
    dk_ref,
    dv_ref,
    loc_q,
    loc_k,
    loc_v,
    loc_g,
    m_out,
    m_got,
    x_out,
    x_got,
    c_out,
    c_got,
    kv,
    kvt,
    qs,
    gs,
    gst,
    s_buf,
    p_buf,
    ds_buf,
    mx,
    peak,
    total,
    factor,
    delta,
    ot,
    attt,
    acc,
    sb,
    rr4,
    rr3,
    rr2,
    rr1,
    load_sem,
    out_sem,
    move_send,
    move_recv,
    halo_send,
    halo_recv,
    back_send,
    back_recv,
):
    s = lax.axis_index("seq")
    h = lax.axis_index("head")
    core = lax.rem(s, 2)
    xhi = lax.rem(lax.div(s, 2), 2)
    up4 = lax.rem(s + 4, NSEQ)
    down4 = lax.rem(s + NSEQ - 4, NSEQ)
    part_x = s + 2 - 4 * xhi
    part_c = s + 1 - 2 * core
    cross = jnp.clip(s - 1 + 2 * core, 0, NSEQ - 1)

    ins = (k_in, v_in, q_in, g_in)
    locs = (loc_k, loc_v, loc_q, loc_g)
    widths = (KW, KW, QW, QW)

    def load(a, half):
        return pltpu.make_async_copy(
            ins[a].at[:, pl.ds(half * widths[a], widths[a])],
            locs[a].at[half],
            load_sem.at[a, half],
        )

    for a in range(4):
        for half in range(2):
            load(a, half).start()

    barrier = pltpu.get_barrier_semaphore()

    def greet(seq, head):
        pl.semaphore_signal(barrier, inc=1, device_id=(seq, head), device_id_type=MESH)

    greet(s, 1 - h)
    greet(cross, 1 - h)
    for other in (part_c, part_x, up4, down4):
        greet(other, h)
    pl.semaphore_wait(barrier, 6)

    crosses = lax.div(home_ref[2 * s + h], 2) != part_c
    told = jnp.where(crosses, h, 1 - h)

    def column(i):
        if i < 2 * KVH:
            return i // KVH, i % KVH
        i -= 2 * KVH
        return 2 + i // QH, i % QH

    pieces = ((0, 1), (1, 2), (2, 3), (3, 4), (4, 8), (8, 12), (12, 16), (16, 20))
    chunks = range(2 * KVH)

    def own(i, half):
        a, c = column(i)
        return locs[a][half, :, pl.ds(c * HEAD, HEAD)]

    def move(way, piece):
        lo, hi = pieces[piece]
        src, dst, to = (
            (m_out, m_got, (s, 1 - h)),
            (x_out, x_got, (cross, 1 - h)),
            (c_out, c_got, (part_c, h)),
        )[way]
        return pltpu.make_async_remote_copy(
            src_ref=src.at[pl.ds(lo, hi - lo)],
            dst_ref=dst.at[pl.ds(lo, hi - lo)],
            send_sem=move_send.at[way, piece],
            recv_sem=move_recv.at[way, piece],
            device_id=to,
            device_id_type=MESH,
        )

    def tell(piece):
        for i in range(*pieces[piece]):
            m_out[i] = own(i, told)
        move(0, piece).start()

    def pass_on(piece):
        move(0, piece).wait_recv()
        for i in range(*pieces[piece]):
            got = m_got[i]
            x_out[i] = lax.select(crosses, own(i, 1 - h), got)
            c_out[i] = lax.select(crosses, got, own(i, h))
        move(1, piece).start()
        move(2, piece).start()

    inside = []
    for p in range(2):
        want = 2 * s + p
        inside.append((home_ref[2 * part_c] == want) | (home_ref[2 * part_c + 1] == want))

    def settle(piece):
        move(1, piece).wait_recv()
        move(2, piece).wait_recv()
        for i in range(*pieces[piece]):
            a, c = column(i)
            for p in range(2):
                block = lax.select(inside[p], c_got[i], x_got[i])
                if a < 2:
                    kv[0, c, a, pl.ds(p * BLK, BLK), :] = block
                else:
                    rows = pl.ds((c % PER) * TOK + p * BLK, BLK)
                    (qs if a == 2 else gs)[c // PER, rows, :] = block

    def halo(src, dst, seq, sem, i):
        g, kind = i % KVH, i // KVH
        return pltpu.make_async_remote_copy(
            src_ref=kv.at[src, g, kind],
            dst_ref=kv.at[dst, g, kind],
            send_sem=halo_send.at[sem, i],
            recv_sem=halo_recv.at[dst, i],
            device_id=(seq, h),
            device_id_type=MESH,
        )

    def have(d, i):
        ref = kv.at[d, i % KVH, i // KVH]
        pltpu.make_async_copy(ref, ref, halo_recv.at[d, i]).wait()

    z0, z4, z2, x0, x4, c0, c2, c4, c6, c8 = (
        [halo(src, dst, seq, sem, i) for i in chunks]
        for sem, (src, dst, seq) in enumerate(
            (
                (0, 4, up4),
                (4, 8, up4),
                (2, 6, up4),
                (0, 2, part_x),
                (4, 2, part_x),
                (0, 1, part_c),
                (2, 3 - 2 * core, part_c),
                (4, 5 - 2 * core, part_c),
                (6, 7 - 2 * core, part_c),
                (8, 7, part_c),
            )
        )
    )

    for a in (0, 1):
        for half in range(2):
            load(a, half).wait()
    for i in chunks:
        tell(i)
    acc[...] = jnp.zeros_like(acc)
    for i in chunks:
        pass_on(i)
    for a in (2, 3):
        for half in range(2):
            load(a, half).wait()
    tell(4)
    tell(5)
    mx[...] = jnp.full_like(mx, LOW)
    for i in chunks:
        settle(i)
        z0[i].start()

        @pl.when(xhi == 0)
        def _():
            x0[i].start()

        @pl.when(core == 0)
        def _():
            c0[i].start()

    def both(step):
        def body(g, carry):
            step(g)
            return carry

        lax.fori_loop(0, KVH, body, 0)

    def turn(d, g):
        cols = pl.ds(PLACE[d] * TOK, TOK)
        for kind in range(2):
            kvt[kind * KVH + g, :, cols] = flip(kv[d, g, kind])

    lane = lax.broadcasted_iota(jnp.int32, (1, TOK), 1)

    def hidden(d, pu):
        back = s - d
        key_doc = doc_ref[jnp.maximum(2 * back + pu, 0)]
        low = []
        for pt in range(2):
            seen = (doc_ref[2 * s + pt] == key_doc) & (back >= 0)
            low.append(jnp.where(seen, 0.0, LOW).astype(F32))
        return jnp.where(lane < BLK, low[0], low[1])

    def held(d):
        i = PLACE[d]
        return (i if i < EARLY else i - EARLY) * TOK

    def score(d, g):
        for j in range(PER):
            cols = pl.ds(j * TOK, TOK)
            tile = dot_nt(kv[d, g, 0], qs[g, cols, :])
            if d in (0, ND - 1):
                row = lax.broadcasted_iota(jnp.int32, (TOK, TOK), 0)
                col = lax.broadcasted_iota(jnp.int32, (TOK, TOK), 1)
                keep = row <= col if d == 0 else row > col
                tile = jnp.where(keep, tile, LOW)
            s_buf[g, pl.ds(held(d), TOK), cols] = tile
            best = mx[g, :, cols]
            for pu in range(2):
                top = jnp.max(tile[pu * BLK : (pu + 1) * BLK].reshape(BLK // 8, 8, TOK), axis=0)
                best = jnp.maximum(best, top + hidden(d, pu))
            mx[g, :, cols] = best

    def weigh(part, g):
        group = ORDER[:EARLY] if part == 0 else ORDER[EARLY:]
        first = 0 if part == 0 else EARLY * TOK
        for j in range(PER):
            cols = pl.ds(j * TOK, TOK)
            top = jnp.max(mx[g, :, cols], axis=0, keepdims=True) * C2
            peak[part, g, :, cols] = top
            added = jnp.zeros((8, TOK), F32)
            for d in group:
                for pu in range(2):
                    base = top - hidden(d, pu)
                    e = jnp.exp2(s_buf[g, pl.ds(held(d) + pu * BLK, BLK), cols] * C2 - base)
                    added = added + jnp.sum(e.reshape(BLK // 8, 8, TOK), axis=0)
                    p_buf[g, pl.ds(PLACE[d] * TOK + pu * BLK, BLK), cols] = e.astype(BF16)
            total[part, g, :, cols] = jnp.sum(added, axis=0, keepdims=True)
            rows = pl.ds(first, len(group) * TOK)
            ot[part, g, :, cols] = dot(kvt[KVH + g, :, rows], p_buf[g, rows, cols])

    def join(g):
        shift = jnp.exp2(peak[0, g] - peak[1, g])
        inv = 1.0 / (total[0, g] * shift + total[1, g])
        factor[0, g] = shift * inv
        factor[1, g] = inv
        a = (ot[0, g] * factor[0, g] + ot[1, g] * inv).astype(BF16)
        attt[g] = a
        for j in range(PER):
            cols = slice(j * TOK, (j + 1) * TOK)
            delta[g, :, cols] = jnp.sum(
                gst[g, :, cols].astype(F32) * a[:, cols].astype(F32), axis=0, keepdims=True
            )

    tell(6)
    tell(7)
    pass_on(4)
    pass_on(5)
    for i in chunks:
        have(4, i)
        z4[i].start()

        @pl.when(xhi == 1)
        def _():
            x4[i].start()

        c4[i].start()
    both(lambda g: turn(0, g))
    both(lambda g: turn(4, g))
    settle(4)
    settle(5)
    both(lambda g: score(0, g))
    both(lambda g: score(4, g))
    for i in chunks:
        have(2, i)
        z2[i].start()
        c2[i].start()
    pass_on(6)
    pass_on(7)
    both(lambda g: turn(2, g))
    both(lambda g: score(2, g))
    for i in chunks:
        have(8, i)

        @pl.when(core == 1)
        def _():
            c8[i].start()

    for d in (8, 1, 3):
        if d < 8:
            for i in chunks:
                have(d, i)
        both(lambda g: turn(d, g))
        both(lambda g: score(d, g))
    weigh(0, 0)
    for i in chunks:
        have(6, i)
        c6[i].start()
    weigh(0, 1)
    both(lambda g: turn(6, g))
    both(lambda g: score(6, g))
    for d in (5, 7):
        for i in chunks:
            have(d, i)
        both(lambda g: turn(d, g))
        both(lambda g: score(d, g))
    settle(6)
    settle(7)

    def finish(g):
        for j in range(PER):
            cols = pl.ds(j * TOK, TOK)
            gst[g, :, cols] = flip(gs[g, cols, :])
        weigh(1, g)
        join(g)

    both(finish)

    def slope(d, g):
        rows = pl.ds(PLACE[d] * TOK, TOK)
        part = 0 if PLACE[d] < EARLY else 1
        for j in range(PER):
            cols = pl.ds(j * TOK, TOK)
            dp = dot(kv[d, g, 1], gst[g, :, cols])
            prob = p_buf[g, rows, cols].astype(F32) * factor[part, g, :, cols]
            p_buf[g, rows, cols] = prob.astype(BF16)
            ds_buf[g, rows, cols] = (prob * (dp - delta[g, :, cols])).astype(BF16)
        acc[d, g, 0] += dot(ds_buf[g, rows, :], qs[g])
        acc[d, g, 1] += dot(p_buf[g, rows, :], gs[g])

    def give(d, dst, seq, sem):
        return [
            pltpu.make_async_remote_copy(
                src_ref=sb.at[d, i % KVH, i // KVH],
                dst_ref=dst.at[i % KVH, i // KVH],
                send_sem=back_send.at[sem, i],
                recv_sem=back_recv.at[sem, i],
                device_id=(seq, h),
                device_id_type=MESH,
            )
            for i in chunks
        ]

    b7 = give(7, rr4.at[3], part_c, 3)
    b5 = give(5, rr4.at[2], part_c, 2)
    b3 = give(3, rr4.at[1], part_c, 1)
    b1 = give(1, rr4.at[0], part_c, 0)
    b6 = give(6, rr3.at[1], down4, 5)
    b2 = give(2, rr3.at[0], part_x, 4)
    b8 = give(8, rr2, down4, 6)
    b4 = give(4, rr1, down4, 7)

    def post(d, copy, i):
        sb[d, i % KVH, i // KVH] = acc[d, i % KVH, i // KVH].astype(BF16)
        copy[i].start()

    def take(copy, ref, d, i):
        copy[i].wait_recv()
        acc[d, i % KVH, i // KVH] += ref[i % KVH, i // KVH].astype(F32)

    def leave(i, ref, out):
        return pltpu.make_async_copy(ref, out, out_sem.at[i])

    outs = [
        leave(i, *pair)
        for i, pair in enumerate(
            ((att_ref, att_out), (dq_ref, dq_out), (dk_ref, dk_out), (dv_ref, dv_out))
        )
    ]

    def kinds(g):
        return (g, g + KVH)

    for d, copy in ((7, b7), (5, b5)):
        for g in range(KVH):
            slope(d, g)
            for i in kinds(g):
                post(d, copy, i)
    for g in range(KVH):
        slope(6, g)
        for i in kinds(g):
            take(b7, rr4.at[3], 6 + 2 * core, i)
            take(b5, rr4.at[2], 4 + 2 * core, i)
            post(6, b6, i)
    for g in range(KVH):
        slope(8, g)
        for i in kinds(g):
            post(8, b8, i)
    for d, copy in ((3, b3), (1, b1)):
        for g in range(KVH):
            slope(d, g)
            for i in kinds(g):
                post(d, copy, i)
    for g in range(KVH):
        slope(2, g)
        for i in kinds(g):
            take(b3, rr4.at[1], 2 + 2 * core, i)
            take(b1, rr4.at[0], 2 * core, i)
            take(b6, rr3.at[1], 2, i)
            post(2, b2, i)
    for g in range(KVH):
        slope(4, g)
        slope(0, g)
    for i in range(QH):
        g, j = i // PER, i % PER
        cols = pl.ds(j * TOK, TOK)
        att_ref[:, pl.ds(i * HEAD, HEAD)] = flip(attt[g, :, cols])
    outs[0].start()
    for i in range(QH):
        g, j = i // PER, i % PER
        term = dot(kvt[g], ds_buf[g, :, pl.ds(j * TOK, TOK)])
        dq_ref[:, pl.ds(i * HEAD, HEAD)] = flip((term * SCALE).astype(BF16))
    outs[1].start()
    for g in range(KVH):
        for i in kinds(g):
            take(b8, rr2, 4, i)
            take(b2, rr3.at[0], 4 * xhi, i)
            post(4, b4, i)
    for g in range(KVH):
        for i in kinds(g):
            take(b4, rr1, 0, i)
        dk_ref[:, pl.ds(g * HEAD, HEAD)] = (acc[0, g, 0] * SCALE).astype(BF16)
        dv_ref[:, pl.ds(g * HEAD, HEAD)] = acc[0, g, 1].astype(BF16)
    outs[2].start()
    outs[3].start()

    for way in range(3):
        for piece in range(len(pieces)):
            move(way, piece).wait_send()
    for copy in (z0, z4, z2, c2, c4, c6, b7, b5, b3, b1, b6, b2, b8, b4):
        for i in chunks:
            copy[i].wait_send()

    for ahead, copy in ((xhi == 0, x0), (xhi == 1, x4), (core == 0, c0), (core == 1, c8)):

        @pl.when(ahead)
        def _():
            for i in chunks:
                copy[i].wait_send()

    for copy in outs:
        copy.wait()


def place_kernel(*refs):
    ins, outs, held, sem = refs[:4], refs[4:8], refs[8:12], refs[12]
    reads = [pltpu.make_async_copy(ins[i], held[i], sem.at[0, i]) for i in range(4)]
    writes = [pltpu.make_async_copy(held[i], outs[i], sem.at[1, i]) for i in range(4)]
    for copy in reads:
        copy.start()
    for read, write in zip(reads, writes):
        read.wait()
        write.start()
    for copy in writes:
        copy.wait()


def per_device(queries, key_states, value_vector_rows, grad_output, doc_ids, block_home):
    smem = pl.BlockSpec(memory_space=pltpu.SMEM)
    anywhere = pl.BlockSpec(memory_space=pl.ANY)
    shapes = (
        jax.ShapeDtypeStruct((TOK, QW), BF16),
        jax.ShapeDtypeStruct((TOK, QW), BF16),
        jax.ShapeDtypeStruct((TOK, KW), BF16),
        jax.ShapeDtypeStruct((TOK, KW), BF16),
    )
    out = pl.pallas_call(
        kernel,
        out_shape=shapes,
        in_specs=[smem, smem, anywhere, anywhere, anywhere, anywhere],
        out_specs=(anywhere, anywhere, anywhere, anywhere),
        scratch_shapes=[
            *[pltpu.VMEM(shape.shape, BF16) for shape in shapes],
            pltpu.VMEM((2, BLK, QW), BF16),
            pltpu.VMEM((2, BLK, KW), BF16),
            pltpu.VMEM((2, BLK, KW), BF16),
            pltpu.VMEM((2, BLK, QW), BF16),
            *[pltpu.VMEM((2 * KVH + 2 * QH, BLK, HEAD), BF16) for _ in range(6)],
            pltpu.VMEM((ND, KVH, 2, TOK, HEAD), BF16),
            pltpu.VMEM((2 * KVH, HEAD, ND * TOK), BF16),
            pltpu.VMEM((KVH, WIDE, HEAD), BF16),
            pltpu.VMEM((KVH, WIDE, HEAD), BF16),
            pltpu.VMEM((KVH, HEAD, WIDE), BF16),
            pltpu.VMEM((KVH, EARLY * TOK, WIDE), F32),
            pltpu.VMEM((KVH, ND * TOK, WIDE), BF16),
            pltpu.VMEM((KVH, ND * TOK, WIDE), BF16),
            pltpu.VMEM((KVH, 8, WIDE), F32),
            pltpu.VMEM((2, KVH, 1, WIDE), F32),
            pltpu.VMEM((2, KVH, 1, WIDE), F32),
            pltpu.VMEM((2, KVH, 1, WIDE), F32),
            pltpu.VMEM((KVH, 1, WIDE), F32),
            pltpu.VMEM((2, KVH, HEAD, WIDE), F32),
            pltpu.VMEM((KVH, HEAD, WIDE), BF16),
            pltpu.VMEM((ND, KVH, 2, TOK, HEAD), F32),
            pltpu.VMEM((ND, KVH, 2, TOK, HEAD), BF16),
            pltpu.VMEM((4, KVH, 2, TOK, HEAD), BF16),
            pltpu.VMEM((2, KVH, 2, TOK, HEAD), BF16),
            pltpu.VMEM((KVH, 2, TOK, HEAD), BF16),
            pltpu.VMEM((KVH, 2, TOK, HEAD), BF16),
            pltpu.SemaphoreType.DMA((4, 2)),
            pltpu.SemaphoreType.DMA((4,)),
            pltpu.SemaphoreType.DMA((3, 8)),
            pltpu.SemaphoreType.DMA((3, 8)),
            pltpu.SemaphoreType.DMA((10, 2 * KVH)),
            pltpu.SemaphoreType.DMA((ND, 2 * KVH)),
            pltpu.SemaphoreType.DMA((8, 2 * KVH)),
            pltpu.SemaphoreType.DMA((8, 2 * KVH)),
        ],
        compiler_params=pltpu.CompilerParams(
            collective_id=0,
            has_side_effects=True,
            vmem_limit_bytes=60 * 1024 * 1024,
        ),
        cost_estimate=pl.CostEstimate(
            flops=8 * 10**9, bytes_accessed=3 * 10**6, transcendentals=5 * 10**6
        ),
    )(doc_ids, block_home, queries, key_states, value_vector_rows, grad_output)
    return pl.pallas_call(
        place_kernel,
        out_shape=shapes,
        in_specs=[anywhere] * 4,
        out_specs=(anywhere,) * 4,
        scratch_shapes=[
            *[pltpu.VMEM(shape.shape, BF16) for shape in shapes],
            pltpu.SemaphoreType.DMA((2, 4)),
        ],
    )(*out)


def solution(mesh):
    return jax.shard_map(
        per_device,
        mesh=mesh,
        in_specs=(
            P(("seq", "head"), None),
            P(("seq", "head"), None),
            P(("seq", "head"), None),
            P(("seq", "head"), None),
            P(),
            P(),
        ),
        out_specs=(P("seq", "head"), P("seq", "head"), P("seq", "head"), P("seq", "head")),
        check_vma=False,
    )
```

time: 92.1 us -> 76.6 us (0.83)
  Pallas kernels: 86.7 us -> 75.7 us
  local copies, waits for them, and re-layouts: 4.56 us -> 0 us
    pallas_call x1 -> x2, Pallas kernels: 86.7 us -> 75.7 us  [the longest x1 73.5 us: per_device(): pl.pallas_call(kernel, out_shape=shapes, in_specs=[smem, smem, anywhere,...]
    unnamed x10 -> x0, local copies, waits for them, and re-layouts: 4.56 us -> none
where the time goes in v3:
time: 76.6 us; the launch traced here: 76.5 us
  Pallas kernels  75.7 us (99%)
  between operations  0.8 us (1%)
    pallas_call x1, Pallas kernels, per_device(): pl.pallas_call(kernel, out_shape=shapes, in_specs=[smem, smem, anywhere,...  73.5 us
    pallas_call x1, Pallas kernels, per_device(): pl.pallas_call(place_kernel, out_shape=shapes, in_specs=[anywhere] * 4, o...  2.16 us

profile of v3, /device:TPU:1, one launch (start us, length us, event | category | flops | bytes accessed | tf_op | source)
XLA Modules:
  0.0 76.5 jit_solution(5011362220618405708)
XLA Ops:
  0.6 73.5 %shard_map.93 = (bf16[256,1024]{1,0:T(8,128)(2,1)}, bf16[256,1024]{1,0:T(8,128)(2,1)}, bf16[256,256]{1,0:T(8,128)(2,1)}, bf16[256,256]{1,0:T(8,128)(2,1)}) custom-call(s32[256]{0:T(256)} %doc_ref.1, s32[256]{0:T(256)} %home_ref.1, bf16[128,2048]{1,0:T(8,128)(2,1)} %q_in.1, bf16[128,512]{1,0:T(8,128)(2,1)} %k_in.1, bf16[128,512]{1,0:T(8,128)(2,1)} %v_in.1, ...), custom_call_target="tpu_custom_call" | custom-call | flops 8000000000 | bytes 3000000 | tf_op jit(solution)/shard_map/pallas_call | solution.py:544
  74.2 2.2 %shard_map.94 = (bf16[256,1024]{1,0:T(8,128)(2,1)}, bf16[256,1024]{1,0:T(8,128)(2,1)}, bf16[256,256]{1,0:T(8,128)(2,1)}, bf16[256,256]{1,0:T(8,128)(2,1)}) custom-call(bf16[256,1024]{1,0:T(8,128)(2,1)} %get-tuple-element.8.refs_0_, bf16[256,1024]{1,0:T(8,128)(2,1)} %get-tuple-element.9.refs_1_, bf16[256,256]{1,0:T(8,128)(2,1)} %get-tuple-element.10.refs_2_, ...), custom_call_target="tpu_custom_call" | custom-call | tf_op jit(solution)/shard_map/pallas_call | solution.py:595

commit v4 on v3

--- a/solution.py
+++ b/solution.py
@@ -143,6 +143,7 @@
 
     pieces = ((0, 1), (1, 2), (2, 3), (3, 4), (4, 8), (8, 12), (12, 16), (16, 20))
     chunks = range(2 * KVH)
+    by_z = (0, KVH)
 
     def own(i, half):
         a, c = column(i)
@@ -263,9 +264,10 @@
         lax.fori_loop(0, KVH, body, 0)
 
     def turn(d, g):
-        cols = pl.ds(PLACE[d] * TOK, TOK)
-        for kind in range(2):
-            kvt[kind * KVH + g, :, cols] = flip(kv[d, g, kind])
+        kvt[KVH + g, :, pl.ds(PLACE[d] * TOK, TOK)] = flip(kv[d, g, 1])
+
+    def turn_key(d, g):
+        kvt[g, :, pl.ds(PLACE[d] * TOK, TOK)] = flip(kv[d, g, 0])
 
     lane = lax.broadcasted_iota(jnp.int32, (1, TOK), 1)
 
@@ -329,8 +331,6 @@
                 gst[g, :, cols].astype(F32) * a[:, cols].astype(F32), axis=0, keepdims=True
             )
 
-    tell(6)
-    tell(7)
     pass_on(4)
     pass_on(5)
     for i in chunks:
@@ -342,6 +342,8 @@
             x4[i].start()
 
         c4[i].start()
+    tell(6)
+    tell(7)
     both(lambda g: turn(0, g))
     both(lambda g: turn(4, g))
     settle(4)
@@ -358,7 +360,6 @@
     both(lambda g: score(2, g))
     for i in chunks:
         have(8, i)
-
         @pl.when(core == 1)
         def _():
             c8[i].start()
@@ -391,8 +392,6 @@
         weigh(1, g)
         join(g)
 
-    both(finish)
-
     def slope(d, g):
         rows = pl.ds(PLACE[d] * TOK, TOK)
         part = 0 if PLACE[d] < EARLY else 1
@@ -405,27 +404,27 @@
         acc[d, g, 0] += dot(ds_buf[g, rows, :], qs[g])
         acc[d, g, 1] += dot(p_buf[g, rows, :], gs[g])
 
-    def give(d, dst, seq, sem):
+    def give(d, dst, seq, seq_x, sem):
         return [
             pltpu.make_async_remote_copy(
                 src_ref=sb.at[d, i % KVH, i // KVH],
                 dst_ref=dst.at[i % KVH, i // KVH],
                 send_sem=back_send.at[sem, i],
                 recv_sem=back_recv.at[sem, i],
-                device_id=(seq, h),
+                device_id=(seq if i in by_z else seq_x, h),
                 device_id_type=MESH,
             )
             for i in chunks
         ]
 
-    b7 = give(7, rr4.at[3], part_c, 3)
-    b5 = give(5, rr4.at[2], part_c, 2)
-    b3 = give(3, rr4.at[1], part_c, 1)
-    b1 = give(1, rr4.at[0], part_c, 0)
-    b6 = give(6, rr3.at[1], down4, 5)
-    b2 = give(2, rr3.at[0], part_x, 4)
-    b8 = give(8, rr2, down4, 6)
-    b4 = give(4, rr1, down4, 7)
+    b7 = give(7, rr4.at[3], part_c, part_c, 3)
+    b5 = give(5, rr4.at[2], part_c, part_c, 2)
+    b3 = give(3, rr4.at[1], part_c, part_c, 1)
+    b1 = give(1, rr4.at[0], part_c, part_c, 0)
+    b6 = give(6, rr3.at[1], down4, part_x, 5)
+    b2 = give(2, rr3.at[0], part_x, part_x, 4)
+    b8 = give(8, rr2, down4, down4, 6)
+    b4 = give(4, rr1, down4, down4, 7)
 
     def post(d, copy, i):
         sb[d, i % KVH, i // KVH] = acc[d, i % KVH, i // KVH].astype(BF16)
@@ -448,36 +447,51 @@
     def kinds(g):
         return (g, g + KVH)
 
-    for d, copy in ((7, b7), (5, b5)):
-        for g in range(KVH):
-            slope(d, g)
-            for i in kinds(g):
-                post(d, copy, i)
-    for g in range(KVH):
+    def near(d, copy, g):
+        slope(d, g)
+        for i in kinds(g):
+            post(d, copy, i)
+
+    def sixth(g):
         slope(6, g)
         for i in kinds(g):
             take(b7, rr4.at[3], 6 + 2 * core, i)
             take(b5, rr4.at[2], 4 + 2 * core, i)
             post(6, b6, i)
-    for g in range(KVH):
-        slope(8, g)
-        for i in kinds(g):
-            post(8, b8, i)
-    for d, copy in ((3, b3), (1, b1)):
-        for g in range(KVH):
-            slope(d, g)
-            for i in kinds(g):
-                post(d, copy, i)
-    for g in range(KVH):
-        slope(2, g)
-        for i in kinds(g):
-            take(b3, rr4.at[1], 2 + 2 * core, i)
-            take(b1, rr4.at[0], 2 * core, i)
-            take(b6, rr3.at[1], 2, i)
-            post(2, b2, i)
-    for g in range(KVH):
-        slope(4, g)
-        slope(0, g)
+
+    finish(0)
+    near(7, b7, 0)
+    near(5, b5, 0)
+    finish(1)
+    near(7, b7, 1)
+    near(5, b5, 1)
+    sixth(0)
+    near(8, b8, 0)
+    near(3, b3, 0)
+    near(1, b1, 0)
+    sixth(1)
+    near(3, b3, 1)
+    near(1, b1, 1)
+    slope(2, 0)
+    slope(8, 1)
+    slope(2, 1)
+    slope(4, 0)
+    for i in kinds(0):
+        take(b3, rr4.at[1], 2 + 2 * core, i)
+        take(b1, rr4.at[0], 2 * core, i)
+        take(b6, rr3.at[1], 2, i)
+        post(2, b2, i)
+    slope(4, 1)
+    for i in kinds(1):
+        take(b3, rr4.at[1], 2 + 2 * core, i)
+        take(b1, rr4.at[0], 2 * core, i)
+        take(b6, rr3.at[1], 4 + 4 * xhi, i)
+        post(8, b8, i)
+        post(2, b2, i)
+    slope(0, 0)
+    slope(0, 1)
+    for d in ORDER:
+        both(lambda g: turn_key(d, g))
     for i in range(QH):
         g, j = i // PER, i % PER
         cols = pl.ds(j * TOK, TOK)

time: 76.6 us -> 72.7 us (0.949)
  Pallas kernels: 75.7 us -> 71.7 us
    pallas_call x1, Pallas kernels: 73.5 us -> 69.5 us  [per_device(): pl.pallas_call(kernel, out_shape=shapes, in_specs=[smem, smem, anywhere,...]
where the time goes in v4:
time: 72.7 us; the launch traced here: 72.5 us
  Pallas kernels  71.7 us (99%)
  between operations  0.8 us (1%)
    pallas_call x1, Pallas kernels, per_device(): pl.pallas_call(kernel, out_shape=shapes, in_specs=[smem, smem, anywhere,...  69.5 us
    pallas_call x1, Pallas kernels, per_device(): pl.pallas_call(place_kernel, out_shape=shapes, in_specs=[anywhere] * 4, o...  2.16 us

profile of v4, /device:TPU:1, one launch (start us, length us, event | category | flops | bytes accessed | tf_op | source)
XLA Modules:
  0.0 72.5 jit_solution(5900357725944361003)
XLA Ops:
  0.6 69.5 %shard_map.93 = (bf16[256,1024]{1,0:T(8,128)(2,1)}, bf16[256,1024]{1,0:T(8,128)(2,1)}, bf16[256,256]{1,0:T(8,128)(2,1)}, bf16[256,256]{1,0:T(8,128)(2,1)}) custom-call(s32[256]{0:T(256)} %doc_ref.1, s32[256]{0:T(256)} %home_ref.1, bf16[128,2048]{1,0:T(8,128)(2,1)} %q_in.1, bf16[128,512]{1,0:T(8,128)(2,1)} %k_in.1, bf16[128,512]{1,0:T(8,128)(2,1)} %v_in.1, ...), custom_call_target="tpu_custom_call" | custom-call | flops 8000000000 | bytes 3000000 | tf_op jit(solution)/shard_map/pallas_call | solution.py:558
  70.2 2.2 %shard_map.94 = (bf16[256,1024]{1,0:T(8,128)(2,1)}, bf16[256,1024]{1,0:T(8,128)(2,1)}, bf16[256,256]{1,0:T(8,128)(2,1)}, bf16[256,256]{1,0:T(8,128)(2,1)}) custom-call(bf16[256,1024]{1,0:T(8,128)(2,1)} %get-tuple-element.8.refs_0_, bf16[256,1024]{1,0:T(8,128)(2,1)} %get-tuple-element.9.refs_1_, bf16[256,256]{1,0:T(8,128)(2,1)} %get-tuple-element.10.refs_2_, ...), custom_call_target="tpu_custom_call" | custom-call | tf_op jit(solution)/shard_map/pallas_call | solution.py:609
